TPU v7x, 128 devices: a whole 4x4x4 slice. The times are simulated.
128 devices in a mesh: side: 2 (over y_hi), expert: 8 (over y_lo, z), tp: 8 (over x, core).
Axes of the slice: x: 4, y: 4 (y_hi: 2, y_lo: 2; y = y_hi * 2 + y_lo), z: 4, core: 2. Of those that a mesh axis runs over, the one named last changes fastest.
Arguments:
- resid: bfloat16 [512, 6144], P(('side', 'expert', 'tp')), may hold values from -6 to 6
- query: bfloat16 [512, 6144], P(('side', 'expert', 'tp')), may hold values from -90 to 90
- key_cache: bfloat16 [512, 128, 1024], P(('side', 'expert', 'tp')), may hold values from -4 to 4
- value_cache: bfloat16 [512, 128, 1024], P(('side', 'expert', 'tp')), may hold values from -6 to 6
- new_key: bfloat16 [512, 1024], P(('side', 'expert', 'tp')), may hold values from -5 to 5
- new_value: bfloat16 [512, 1024], P(('side', 'expert', 'tp')), may hold values from -5 to 5
- cache_len: int32 [512], P(('side', 'expert', 'tp')), may hold values from 2 to 128, as said below
- norm_gain: float32 [6144], replicated, may hold values from 0.1 to 1.9
- routes: int32 [512, 4], P(('side', 'expert')), may hold values from 0 to 15, all different within a row; in each aligned block of 4 rows (0 to 3, 4 to 7, ...) at most 2 rows name the same one
- gate_fixed: int32 [512, 4], P(('side', 'expert')), may hold values from 1 to 4095
- w_gate: bfloat16 [16, 5376, 6144], P(('side', 'expert'), 'tp'), may hold values from -0.078125 to 0.078125
- w_up: bfloat16 [16, 5376, 6144], P(('side', 'expert'), 'tp'), may hold values from -0.078125 to 0.078125
- w_down: bfloat16 [16, 5376, 6144], P(('side', 'expert'), 'tp'), may hold values from -0.078125 to 0.078125
Outputs:
- layer_out: bfloat16 [512, 6144], P(('side', 'expert', 'tp'))
Inputs may be any that keep to these rules, and one draw needn't show every extreme that they name: `cache_len`: a row's cache holds at least 2 valid positions; in every draw all rows of some device hold 128. `routes`: each row names 4 different experts; within the rows of one device no expert is named by more than 2 rows, a bound that some block reaches.
All inputs are finite; a program needn't handle non-finite values.
Results may differ from a plain program's by a relative error of at most 0.007.
Values may be sent and summed in bfloat16 or wider, within the bound.
A program may use at most 128 MiB of HBM per device.

v0:
```python
import jax
import jax.numpy as jnp
from jax import lax
from jax.sharding import PartitionSpec as P

D = 6144
HEADS = 48
KV_HEADS = 8
HEAD_DIM = 128


def attend(resid, query, key_cache, value_cache, new_key, new_value, cache_len):
    count = resid.shape[0]
    length = key_cache.shape[1]
    group = HEADS // KV_HEADS
    scale = 1.0 / HEAD_DIM**0.5
    q = query.reshape(count, KV_HEADS, group, HEAD_DIM)
    keys = key_cache.reshape(count, length, KV_HEADS, HEAD_DIM)
    values = value_cache.reshape(count, length, KV_HEADS, HEAD_DIM)
    knew = new_key.reshape(count, KV_HEADS, HEAD_DIM)
    vnew = new_value.reshape(count, KV_HEADS, HEAD_DIM)
    scores = jnp.einsum("rkgd,rpkd->rkgp", q, keys, preferred_element_type=jnp.float32) * scale
    own = jnp.einsum("rkgd,rkd->rkg", q, knew, preferred_element_type=jnp.float32) * scale
    valid = jnp.arange(length, dtype=jnp.int32)[None, :] < cache_len[:, None]
    scores = jnp.where(valid[:, None, None, :], scores, -1e30)
    top = jnp.maximum(jnp.max(scores, axis=-1), own)
    expo = jnp.exp(scores - top[..., None])
    expo_own = jnp.exp(own - top)
    total = jnp.sum(expo, axis=-1) + expo_own
    probs = (expo / total[..., None]).astype(jnp.bfloat16)
    prob_own = (expo_own / total).astype(jnp.bfloat16)
    attn = jnp.einsum("rkgp,rpkd->rkgd", probs, values, preferred_element_type=jnp.float32)
    attn = attn + prob_own.astype(jnp.float32)[..., None] * vnew.astype(jnp.float32)[:, :, None, :]
    return resid.astype(jnp.float32) + attn.reshape(count, D)


def normalize(stream, norm_gain):
    mean = jnp.mean(stream, axis=-1, keepdims=True)
    centred = stream - mean
    variance = jnp.mean(centred * centred, axis=-1, keepdims=True)
    return (centred * lax.rsqrt(variance + 1e-05) * norm_gain).astype(jnp.bfloat16)


def expert_ffn(arrived, w_gate, w_up, w_down):
    flat = arrived.reshape(-1, arrived.shape[-1])
    dims = (((1,), (1,)), ((), ()))
    gate = lax.dot_general(flat, w_gate[0], dims, preferred_element_type=jnp.float32)
    upper = lax.dot_general(flat, w_up[0], dims, preferred_element_type=jnp.float32)
    hidden = (jax.nn.silu(gate) * upper).astype(jnp.bfloat16)
    output = jnp.dot(hidden, w_down[0], preferred_element_type=jnp.float32)
    return output.reshape(arrived.shape[0], arrived.shape[1], -1)


def slot_targets(route_rows, owner, capacity):
    flat_routes = route_rows.reshape(-1)
    onehot = (flat_routes[:, None] == owner[None, :]).astype(jnp.int32)
    before = jnp.cumsum(onehot, axis=0) - onehot
    slot = jnp.sum(before * onehot, axis=1)
    return (flat_routes * capacity + slot).reshape(route_rows.shape[0], -1)


def shards(
    resid,
    query,
    key_cache,
    value_cache,
    new_key,
    new_value,
    cache_len,
    norm_gain,
    routes,
    gate_fixed,
    w_gate,
    w_up,
    w_down,
):
    count = resid.shape[0]
    stream = attend(resid, query, key_cache, value_cache, new_key, new_value, cache_len)
    moe_in = normalize(stream, norm_gain)
    fixed = gate_fixed.astype(jnp.float32)
    weights = fixed / jnp.sum(fixed, axis=-1, keepdims=True)
    experts = lax.axis_size("side") * lax.axis_size("expert")
    slices = lax.axis_size("tp")
    owner = jnp.arange(experts, dtype=jnp.int32)
    start = lax.axis_index("tp") * count
    my_routes = lax.dynamic_slice_in_dim(routes, start, count, 0)
    my_weights = lax.dynamic_slice_in_dim(weights, start, count, 0)
    capacity = count // 2
    target = slot_targets(my_routes, owner, capacity)
    places = jnp.arange(experts * capacity, dtype=jnp.int32)
    select = jnp.any(places[:, None, None] == target[None], axis=-1).astype(jnp.bfloat16)
    packed = jnp.dot(select, moe_in, preferred_element_type=jnp.float32).astype(jnp.bfloat16)
    packed = packed.reshape(experts, 1, capacity, D)
    outgoing = jnp.broadcast_to(packed, (experts, slices, capacity, D))
    outgoing = outgoing.reshape(experts * slices, capacity, D)
    partial_out = expert_ffn(
        lax.all_to_all(outgoing, ("side", "expert", "tp"), split_axis=0, concat_axis=0, tiled=True),
        w_gate,
        w_up,
        w_down,
    )
    returned = lax.all_to_all(
        partial_out.astype(jnp.bfloat16),
        ("side", "expert", "tp"),
        split_axis=0,
        concat_axis=0,
        tiled=True,
    ).astype(partial_out.dtype)
    summed = jnp.sum(returned.reshape(experts, slices, capacity, D), axis=1)
    combine = jnp.sum(
        jnp.where(places[None, None, :] == target[:, :, None], my_weights[:, :, None], 0.0), axis=1
    )
    moe = jnp.dot(
        combine,
        summed.reshape(experts * capacity, D),
        precision=lax.Precision.HIGHEST,
        preferred_element_type=jnp.float32,
    )
    return (stream + moe).astype(jnp.bfloat16)


def solution(mesh):
    placed = (
        P(("side", "expert", "tp"), None),
        P(("side", "expert", "tp"), None),
        P(("side", "expert", "tp"), None, None),
        P(("side", "expert", "tp"), None, None),
        P(("side", "expert", "tp"), None),
        P(("side", "expert", "tp"), None),
        P(("side", "expert", "tp")),
        P(),
        P(("side", "expert"), None),
        P(("side", "expert"), None),
        P(("side", "expert"), "tp", None),
        P(("side", "expert"), "tp", None),
        P(("side", "expert"), "tp", None),
    )
    return jax.shard_map(
        shards,
        mesh=mesh,
        in_specs=placed,
        out_specs=P(("side", "expert", "tp"), None),
        check_vma=False,
    )
```

profile of v0, /device:TPU:0, one launch (start us, length us, event | category | flops | bytes accessed | tf_op | source)
XLA Modules:
  0.0 150.5 jit_solution(16736227036887359931)
XLA Ops:
  0.0 0.8 iota_compare_fusion.3
  0.8 0.8 constant_dynamic-slice_fusion.1
  1.6 0.1 copy.54
  1.9 0.2 select_reduce_fusion.1
  2.1 0.1 fusion.30
  2.2 0.7 reshape.108
  3.0 0.7 convert_bitcast_fusion
  3.7 0.9 reshape.91
  4.5 0.1 fusion.34
  4.7 0.7 fusion.33
  5.4 0.2 fusion.22
  5.7 1.7 %convolution_add_fusion.1 = f32[4,8,6,128]{3,2,1,0:T(8,128)S(1)} fusion(f32[4,8,6,128]{3,2,1,0:T(8,128)S(1)} %get-tuple-element.8, f32[4,8,128]{2,1,0:T(8,128)S(1)} %bitcast.54, f32[4,8,6]{2,1,0:T(8,128)S(1)} %get-tuple-element.6, f32[4,8,6]{2,1,0:T(8,128)S(1)} %get-tuple-element.5, f32[4,8,6]{2,1,0:T(8,128)S(1)} %multiply_maximum_fusion, ...), kind=kOutput, calls=%fused_computation.13 | convolution fusion | flops 6414336 | bytes 1263872 | tf_op jit(solution)/shard_map/rkgp,rpkd->rkgd/dot_general | solution.py:32
  7.4 1.0 fusion.32
  8.4 1.0 multiply_reduce_fusion
  9.4 1.1 convolution_convert_fusion
  10.6 0.3 broadcast_in_dim.28
  10.8 1.9 %broadcast_in_dim.29 = bf16[16,8,2,6144]{3,2,1,0:T(2,128)(2,1)S(1)} broadcast(bf16[16,2,6144]{2,1,0:T(2,128)(2,1)S(1)} %broadcast_in_dim.28), dimensions={0,2,3} | broadcast | bytes 3538944 | tf_op jit(solution)/shard_map/broadcast_in_dim | solution.py:94
  12.7 52.7 %all_to_all.10 = bf16[128,2,6144]{2,1,0:T(2,128)(2,1)} all-to-all(bf16[128,2,6144]{2,1,0:T(2,128)(2,1)S(1)} %bitcast.51), channel_id=1, replica_groups=mesh['side'=2,'expert'=8,'tp'=8] {'side','expert','tp'}, dimensions={0} | all-to-all | bytes 6291456 | tf_op jit(solution)/shard_map/all_to_all | solution.py:97
  65.4 7.3 %reshape.97 = bf16[256,6144]{1,0:T(8,128)(2,1)} reshape(bf16[128,2,6144]{2,1,0:T(2,128)(2,1)} %all_to_all.10) | data formatting | bytes 6291456 | tf_op jit(solution)/shard_map/reshape | solution.py:45
  72.7 6.8 %fusion.4 = f32[256,672]{0,1:T(8,128)S(1)} fusion(bf16[256,6144]{1,0:T(8,128)(2,1)} %reshape.97, bf16[1,672,6144]{2,1,0:T(8,128)(2,1)} %param.23), kind=kOutput, calls=%fused_computation.4 | convolution fusion | flops 2113929216 | bytes 12091392 | tf_op jit(solution)/shard_map/dot_general | solution.py:47
  79.5 5.7 %fusion.13 = bf16[256,672]{0,1:T(8,128)(2,1)S(1)} fusion(bf16[256,6144]{1,0:T(8,128)(2,1)S(1)} %copy-done.1, bf16[1,672,6144]{2,1,0:T(8,128)(2,1)} %param.24, f32[256,672]{0,1:T(8,128)S(1)} %fusion.4), kind=kOutput, calls=%fused_computation.12 | convolution fusion | flops 2114961408 | bytes 12435456 | tf_op jit(solution)/shard_map/dot_general | solution.py:48
  85.2 0.2 copy.46
  85.4 0.2 dot_general.32
  85.5 6.2 %fusion.6 = bf16[128,2,6144]{2,0,1:T(8,128)(2,1)S(1)} fusion(bf16[1,672,6144]{2,1,0:T(8,128)(2,1)} %param.25, bf16[128,2,672]{2,1,0:T(2,128)(2,1)S(1)} %dot_general.32), kind=kOutput, calls=%fused_computation.6 | convolution fusion | flops 2115502080 | bytes 11747328 | tf_op jit(solution)/shard_map/dot_general | solution.py:50
  91.7 4.9 %copy.48 = bf16[128,2,6144]{2,1,0:T(2,128)(2,1)} copy(bf16[128,2,6144]{2,0,1:T(8,128)(2,1)S(1)} %fusion.6) | data formatting | bytes 6291456 | tf_op jit(solution)/shard_map/convert_element_type | solution.py:103
  96.7 6.1 %all-to-all-start.1 = ((bf16[128,2,6144]{2,1,0:T(2,128)(2,1)}), bf16[128,2,6144]{2,1,0:T(2,128)(2,1)}, u32[]{:S(2)}, u32[]{:S(2)}) async-start(bf16[128,2,6144]{2,1,0:T(2,128)(2,1)} %copy.48), calls=%async_computation.1 | async-start | bytes 6291456 | tf_op jit(solution)/shard_map/all_to_all | solution.py:102
  102.9 0.1 copy.45
  103.0 0.1 select_reduce_fusion
  103.1 40.7 %all-to-all-done.1 = bf16[128,2,6144]{2,1,0:T(2,128)(2,1)} async-done(((bf16[128,2,6144]{2,1,0:T(2,128)(2,1)}), bf16[128,2,6144]{2,1,0:T(2,128)(2,1)}, u32[]{:S(2)}, u32[]{:S(2)}) %all-to-all-start.1) | async-done | bytes 3145760 | tf_op jit(solution)/shard_map/all_to_all | solution.py:102
  143.8 5.0 %convert_reduce_fusion = f32[16,2,6144]{2,1,0:T(2,128)S(1)} fusion(bf16[128,2,6144]{2,1,0:T(2,128)(2,1)} %all-to-all-done.1), kind=kLoop, calls=%fused_computation.10 | loop fusion | flops 2949120 | bytes 3932160 | tf_op jit(solution)/shard_map/reduce_sum | solution.py:109
  148.9 0.5 reshape.100
  149.4 1.1 fusion.9
  (22 shorter events, 0.5 us)
Async XLA Ops:
  0.0 4.7 %copy-start = (bf16[4,128,1024]{2,1,0:T(8,128)(2,1)S(1)}, bf16[4,128,1024]{2,1,0:T(8,128)(2,1)}, u32[]{:S(2)}) copy-start(bf16[4,128,1024]{2,1,0:T(8,128)(2,1)} %param.15) | copy-start | bytes 3145732
  72.7 6.8 %copy-start.1 = (bf16[256,6144]{1,0:T(8,128)(2,1)S(1)}, bf16[256,6144]{1,0:T(8,128)(2,1)}, u32[]{:S(2)}) copy-start(bf16[256,6144]{1,0:T(8,128)(2,1)} %reshape.97) | copy-start | bytes 9437188
  91.7 11.0 %copy-start.3 = (s32[32,4]{0,1:T(4,128)S(1)}, s32[32,4]{0,1:T(4,128)}, u32[]{:S(2)}) copy-start(s32[32,4]{0,1:T(4,128)} %param.22) | copy-start | bytes 1540
  96.7 52.7 %copy-start.2 = (bf16[4,6144]{1,0:T(4,128)(2,1)S(1)}, bf16[4,6144]{1,0:T(4,128)(2,1)}, u32[]{:S(2)}) copy-start(bf16[4,6144]{1,0:T(4,128)(2,1)} %param.13) | copy-start | bytes 147460
  96.7 47.1 %all-to-all-start.1 = ((bf16[128,2,6144]{2,1,0:T(2,128)(2,1)}), bf16[128,2,6144]{2,1,0:T(2,128)(2,1)}, u32[]{:S(2)}, u32[]{:S(2)}) async-start(bf16[128,2,6144]{2,1,0:T(2,128)(2,1)} %copy.48), calls=%async_computation.1 | async-start | bytes 6291456 | tf_op jit(solution)/shard_map/all_to_all | solution.py:102
where the time goes:
time: 152 us; the launch traced here: 151 us
  blocking collectives  52.7 us (35%)
  waiting for transfers between devices  40.7 us (27%)
  matrix products  23.4 us (15%)
  local copies, waits for them, and re-layouts  18.1 us (12%)
  other arithmetic  9.34 us (6%)
  starting transfers between devices  6.08 us (4%)
    all_to_all x1, blocking collectives, shards(): lax.all_to_all(outgoing, ('side', 'expert', 'tp'), split_axis=0, concat_a...  52.7 us
    all_to_all x1, waiting for transfers between devices, shards(): lax.all_to_all(partial_out.astype(jnp.bfloat16), ('side', 'expert', 'tp')...  40.7 us
    reshape x1, local copies, waits for them, and re-layouts, expert_ffn(): flat = arrived.reshape(-1, arrived.shape[-1])  7.33 us
    dot_general x1, matrix products, expert_ffn(): lax.dot_general(flat, w_gate[0], dims, preferred_element_type=jnp.float32)  6.77 us
    dot_general x1, matrix products, expert_ffn(): output = jnp.dot(hidden, w_down[0], preferred_element_type=jnp.float32)  6.18 us
    all_to_all x1, starting transfers between devices, shards(): lax.all_to_all(partial_out.astype(jnp.bfloat16), ('side', 'expert', 'tp')...  6.08 us
    dot_general x1, matrix products, expert_ffn(): lax.dot_general(flat, w_up[0], dims, preferred_element_type=jnp.float32)  5.69 us
    reduce_sum x1, other arithmetic, shards(): summed = jnp.sum(returned.reshape(experts, slices, capacity, D), axis=1)  5.05 us
  transfers between devices with their start and end apart: 1, of which 1 were waited for; matrix products, arithmetic and copies ran while one was open for 0% of the time, Pallas kernels for 0%

commit v1 on v0

v1 whole, which is shorter than its diff:
```python
import functools

import jax
import jax.numpy as jnp
from jax import lax
from jax.experimental import pallas as pl
from jax.experimental.pallas import tpu as pltpu
from jax.sharding import PartitionSpec as P

D = 6144
HEADS = 48
KV_HEADS = 8
HEAD_DIM = 128
GROUP = HEADS // KV_HEADS
ROWS = 4
LENGTH = 128
HIDDEN = 672
CHUNK = 1024
A_CHUNKS = 4
A_COLS = A_CHUNKS * CHUNK
F32 = jnp.float32
BF16 = jnp.bfloat16
MESH = pl.DeviceIdType.MESH
W_PARTS = 3
W_ROWS = HIDDEN // W_PARTS


def iota(shape, dim):
    return lax.broadcasted_iota(jnp.int32, shape, dim)


def dot(a, b):
    return lax.dot_general(a, b, (((1,), (0,)), ((), ())), preferred_element_type=F32)


def dot_nt(a, b):
    return lax.dot_general(a, b, (((1,), (1,)), ((), ())), preferred_element_type=F32)


def onehot(condition):
    return jnp.where(condition, 1.0, 0.0).astype(BF16)


def remote(src, dst, send_sem, recv_sem, device):
    return pltpu.make_async_remote_copy(
        src_ref=src,
        dst_ref=dst,
        send_sem=send_sem,
        recv_sem=recv_sem,
        device_id=device,
        device_id_type=MESH,
    )


def kernel(
    clen,
    resid,
    query,
    new_key,
    new_value,
    gain,
    routes,
    gates,
    key_hbm,
    value_hbm,
    wg_hbm,
    wu_hbm,
    wd_hbm,
    out,
    kbuf,
    vbuf,
    wg,
    wu,
    wd,
    qs,
    scores,
    own_key,
    own_value,
    heads_out,
    stream,
    xs,
    apack,
    arecv,
    bmsg,
    xb1,
    bpack,
    xbh,
    xa,
    accg,
    accu,
    hid,
    hidb,
    pa,
    pm,
    cr,
    cs,
    far,
    near,
    y2,
    asend,
    aback,
    pbs,
    pbm,
    cbr,
    bsend,
    bback,
    fsend,
    frecv,
    local_sem,
    a1s,
    a1r,
    b1s,
    b1r,
    b2s,
    b2r,
    bcs,
    bcr,
    ns,
    nr,
    fs,
    fr,
    acs,
    acr,
    rcs,
    rcr,
    rfs,
    rfr,
    rns,
    rnr,
    ras,
    rar,
    rbcs,
    rbcr,
    rbs,
    rbr,
    rfis,
    rfir,
):
    side = lax.axis_index("side")
    expert = lax.axis_index("expert")
    tp = lax.axis_index("tp")
    me = side * 8 + expert
    my_y = me // 4
    my_z = me % 4
    x = tp // 2
    core = tp % 2
    right = lax.rem(x + 1, 4)
    left = lax.rem(x + 3, 4)
    opposite = lax.rem(x + 2, 4)
    other_dev = (side, expert, x * 2 + 1 - core)
    right_dev = (side, expert, right * 2 + core)
    left_dev = (side, expert, left * 2 + core)

    def plane(step):
        y = lax.rem(my_y + step // 4, 4)
        z = lax.rem(my_z + step % 4, 4)
        peer = y * 4 + z
        return peer, (peer // 8, peer % 8, tp)

    def column(step):
        peer = lax.rem(tp + step, 8)
        return peer, (side, expert, peer)

    barrier = pltpu.get_barrier_semaphore()

    def greet_plane(step, carry):
        pl.semaphore_signal(barrier, inc=1, device_id=plane(step)[1], device_id_type=MESH)
        return carry

    def greet_column(step, carry):
        pl.semaphore_signal(barrier, inc=1, device_id=column(step)[1], device_id_type=MESH)
        return carry

    key_copy = pltpu.make_async_copy(key_hbm, kbuf, local_sem.at[0])
    value_copy = pltpu.make_async_copy(value_hbm, vbuf, local_sem.at[1])
    key_copy.start()
    value_copy.start()
    weight_copies = []
    for number, (src, dst) in enumerate(((wg_hbm, wg), (wu_hbm, wu), (wd_hbm, wd))):
        for part in range(W_PARTS):
            rows = pl.ds(part * W_ROWS, W_ROWS)
            weight_copies.append(
                pltpu.make_async_copy(
                    src.at[0, rows, :],
                    dst.at[rows, :],
                    local_sem.at[2 + number * W_PARTS + part],
                )
            )
    for copy in weight_copies:
        copy.start()
    lax.fori_loop(1, 16, greet_plane, 0)
    lax.fori_loop(1, 8, greet_column, 0)

    q32 = query[...].astype(F32)
    for head in range(HEADS):
        qs[head * 4 : head * 4 + 4, :] = q32[:, head * 128 : head * 128 + 128]
    nk32 = new_key[...].astype(F32)
    nv32 = new_value[...].astype(F32)
    for copy_no in range(GROUP):
        own_key[copy_no * 4 : copy_no * 4 + 4, :] = nk32
        own_value[copy_no * 4 : copy_no * 4 + 4, :] = nv32
    block = GROUP * ROWS
    row_of = iota((block, 128), 0) & 3
    key_copy.wait()
    for j in range(KV_HEADS):
        qj = qs[j * block : (j + 1) * block, :].astype(BF16)
        total = jnp.zeros((block, 128), F32)
        for r in range(ROWS):
            part = dot_nt(qj, kbuf[r, :, j * 128 : (j + 1) * 128])
            total = jnp.where(row_of == r, part, total)
        scores[j * block : (j + 1) * block, :] = total

    lane32 = iota((32, 32), 1)
    row32 = iota((32, 32), 0)
    fixed = gates[...].astype(F32)
    weights = fixed / jnp.sum(fixed, axis=-1, keepdims=True)
    chosen = jnp.zeros((32, 32), F32)
    weighted = jnp.zeros((32, 32), F32)
    route = routes[...]
    for k in range(4):
        same = route[:, k : k + 1] == (lane32 >> 1)
        chosen = chosen + jnp.where(same, 1.0, 0.0)
        weighted = weighted + jnp.where(same, weights[:, k : k + 1], 0.0)
    earlier = onehot(((row32 >> 2) == (lane32 >> 2)) & (lane32 < row32))
    before = dot(earlier, chosen.astype(BF16))
    picked = (chosen > 0.5) & (jnp.abs(before - (lane32 & 1).astype(F32)) < 0.5)
    sel = onehot(picked)
    wsel = jnp.where(picked, weighted, 0.0)
    whi = wsel.astype(BF16)
    wlo = (wsel - whi.astype(F32)).astype(BF16)

    rr = iota((256, 32), 0)
    ll = iota((256, 32), 1)
    spread_a = onehot((rr >> 3) == ll)
    spread_b = onehot(ll == ((rr >> 4) * 2 + (rr & 1)))
    rr = iota((96, 32), 0)
    ll = iota((96, 32), 1)
    mine = onehot((ll == tp * 4 + (rr & 7)) & ((rr & 7) < 4))
    rr = iota((128, 32), 0)
    ll = iota((128, 32), 1)
    wide = onehot(ll == ((rr >> 4) * 4 + (rr & 3)))
    pack_a = dot_nt(spread_a, dot(mine, sel).astype(BF16))
    rr = iota((256, 96), 0)
    ll = iota((256, 96), 1)
    pack_a = jnp.where((rr & 7) == (ll >> 3), pack_a, 0.0).astype(BF16)
    rr = iota((16, 96), 0)
    ll = iota((16, 96), 1)
    pack_b1 = onehot(ll == (8 + (rr >> 2)) * 8 + (rr & 3))
    pack_b = dot_nt(spread_b, dot(wide, sel).astype(BF16))
    rr = iota((256, 128), 0)
    ll = iota((256, 128), 1)
    pack_b = jnp.where(((rr & 15) >> 1) == (ll >> 4), pack_b, 0.0)

    pos = iota((HEADS * ROWS, 128), 1)
    row_all = iota((HEADS * ROWS, 128), 0) & 3
    limit = jnp.zeros((HEADS * ROWS, 128), jnp.int32)
    for r in range(ROWS):
        limit = jnp.where(row_all == r, clen[r], limit)
    scale = 1.0 / HEAD_DIM**0.5
    s = jnp.where(pos < limit, scores[...] * scale, -1e30)
    own = jnp.concatenate(
        [
            jnp.sum(
                qs[j * block : (j + 1) * block, :] * own_key[:, j * 128 : (j + 1) * 128],
                axis=-1,
                keepdims=True,
            )
            for j in range(KV_HEADS)
        ],
        axis=0,
    )
    own = own * scale
    top = jnp.maximum(jnp.max(s, axis=-1, keepdims=True), own)
    expo = jnp.exp(s - top)
    expo_own = jnp.exp(own - top)
    total = jnp.sum(expo, axis=-1, keepdims=True) + expo_own
    scores[...] = expo / total
    prob_own = (expo_own / total).astype(BF16).astype(F32)
    value_copy.wait()
    for j in range(KV_HEADS):
        pj = scores[j * block : (j + 1) * block, :]
        acc = prob_own[j * block : (j + 1) * block, :] * own_value[:, j * 128 : (j + 1) * 128]
        for r in range(ROWS):
            pr = jnp.where(row_of == r, pj, 0.0).astype(BF16)
            acc = acc + dot(pr, vbuf[r, :, j * 128 : (j + 1) * 128])
        heads_out[j * block : (j + 1) * block, :] = acc
    stream[...] = jnp.zeros((8, D), F32)
    for head in range(HEADS):
        cols = slice(head * 128, head * 128 + 128)
        stream[0:4, cols] = resid[:, cols].astype(F32) + heads_out[head * 4 : head * 4 + 4, :]
    st = stream[...]
    mean = jnp.sum(st, axis=-1, keepdims=True) * (1.0 / D)
    centred = st - mean
    variance = jnp.sum(centred * centred, axis=-1, keepdims=True) * (1.0 / D)
    normed = centred * lax.rsqrt(variance + 1e-05) * gain[...]
    for p in range(12):
        xs[p * 8 : p * 8 + 8, :] = normed[:, p * 512 : (p + 1) * 512]
    xbf = xs[...].astype(BF16)

    bm = dot(pack_b1, xbf).astype(BF16)
    bmsg[...] = bm
    xb1[tp] = bm
    pl.semaphore_wait(barrier, 22)

    def send_b1(step, carry):
        peer, device = column(step)
        remote(bmsg, xb1.at[tp], b1s.at[step], b1r.at[tp], device).start()
        return carry

    lax.fori_loop(1, 8, send_b1, 0)
    packed = dot(pack_a, xbf).astype(BF16)
    apack[...] = packed.reshape(16, 16, 512)
    arecv[me] = apack[me]

    def send_a1(step, carry):
        peer, device = plane(step)
        remote(apack.at[peer], arecv.at[me], a1s.at[step], a1r.at[me], device).start()
        return carry

    lax.fori_loop(1, 16, send_a1, 0)

    def wait_b1(step, carry):
        peer, device = column(step)
        remote(bmsg, xb1.at[peer], b1s.at[step], b1r.at[peer], device).wait_recv()
        return carry

    lax.fori_loop(1, 8, wait_b1, 0)
    xb_all = xb1[...].reshape(128, 512)
    for i in range(2):
        pick = jnp.where(((ll & 15) >> 2) == core * 2 + i, pack_b, 0.0).astype(BF16)
        bpack[:, :, i * 512 : (i + 1) * 512] = (
            dot(pick, xb_all).astype(BF16).reshape(16, 16, 512)
        )
    xbh[core, me] = bpack[me]

    def send_b2(step, carry):
        peer, device = plane(step)
        remote(bpack.at[peer], xbh.at[core, me], b2s.at[step], b2r.at[me], device).start()
        return carry

    lax.fori_loop(1, 16, send_b2, 0)

    def wait_a1(step, carry):
        peer, device = plane(step)
        remote(apack.at[peer], arecv.at[peer], a1s.at[step], a1r.at[peer], device).wait_recv()
        return carry

    lax.fori_loop(1, 16, wait_a1, 0)
    rr = iota((256, 256), 0)
    ll = iota((256, 256), 1)
    unpack_a = onehot(ll == (rr & 31) * 8 + (rr >> 5))
    got = dot(unpack_a, arecv[...].reshape(256, 512)).astype(BF16)
    for p in range(8):
        xa[p // 2, core, x, :, (p % 2) * 512 : (p % 2) * 512 + 512] = got[p * 32 : p * 32 + 32, :]

    def near_in(n):
        mine_ref = xa.at[n, core, x]
        to_right = remote(mine_ref, mine_ref, ns.at[0, n], nr.at[0, n], right_dev)
        to_left = remote(mine_ref, mine_ref, ns.at[1, n], nr.at[1, n], left_dev)
        return to_right, to_left

    def near_arrivals(n):
        from_left = xa.at[n, core, left]
        from_right = xa.at[n, core, right]
        a = remote(from_left, from_left, ns.at[0, n], nr.at[0, n], right_dev)
        b = remote(from_right, from_right, ns.at[1, n], nr.at[1, n], left_dev)
        return a, b

    def far_sends(n):
        low = xa.at[n, core, left, pl.ds(0, 16), :]
        high = xa.at[n, core, right, pl.ds(16, 16), :]
        a = remote(low, low, fs.at[0, n], fr.at[0, n], right_dev)
        b = remote(high, high, fs.at[1, n], fr.at[1, n], left_dev)
        return a, b

    def far_arrivals(n):
        low = xa.at[n, core, opposite, pl.ds(0, 16), :]
        high = xa.at[n, core, opposite, pl.ds(16, 16), :]
        a = remote(low, low, fs.at[0, n], fr.at[0, n], right_dev)
        b = remote(high, high, fs.at[1, n], fr.at[1, n], left_dev)
        return a, b

    def core_send(n):
        half = xa.at[n, core]
        return remote(half, half, acs.at[n], acr.at[n], other_dev)

    def core_arrival(n):
        half = xa.at[n, 1 - core]
        return remote(half, half, acs.at[n], acr.at[n], other_dev)

    for n in range(A_CHUNKS):
        for copy in near_in(n):
            copy.start()

    accg[...] = jnp.zeros((256, HIDDEN), F32)
    accu[...] = jnp.zeros((256, HIDDEN), F32)
    for copy in weight_copies[: 2 * W_PARTS]:
        copy.wait()

    def project(value, offset):
        cols = pl.ds(offset, CHUNK)
        accg[...] += dot_nt(value, wg[:, cols])
        accu[...] += dot_nt(value, wu[:, cols])

    def project_a(n):
        core_arrival(n).wait_recv()
        project(xa[n].reshape(256, CHUNK), n * CHUNK)

    def relay(n):
        for copy in near_arrivals(n):
            copy.wait_recv()
        for copy in far_sends(n):
            copy.start()

    def forward(n):
        for copy in far_arrivals(n):
            copy.wait_recv()
        core_send(n).start()

    relay(0)
    relay(1)
    forward(0)
    relay(2)
    forward(1)
    project_a(0)

    def wait_b2(step, carry):
        peer, device = plane(step)
        remote(
            bpack.at[peer], xbh.at[core, peer], b2s.at[step], b2r.at[peer], device
        ).wait_recv()
        return carry

    lax.fori_loop(1, 16, wait_b2, 0)
    bcore = remote(xbh.at[core], xbh.at[core], bcs, bcr, other_dev)
    bcore.start()
    relay(3)
    forward(2)
    project_a(1)
    forward(3)
    remote(xbh.at[1 - core], xbh.at[1 - core], bcs, bcr, other_dev).wait_recv()
    tau = rr >> 5
    unpack_b = onehot(
        ll == ((rr & 31) >> 1) * 16 + ((tau & 3) * 2 + (tau >> 2)) * 2 + (rr & 1)
    )
    for h in range(2):
        project(
            dot(unpack_b, xbh[h].reshape(256, CHUNK)).astype(BF16), A_COLS + h * CHUNK
        )
    project_a(2)
    project_a(3)
    g = accg[...]
    hidden = (g * jax.nn.sigmoid(g) * accu[...]).astype(BF16)
    hid[...] = hidden
    t_of = (rr & 15) >> 1
    to_b = onehot(ll == ((t_of & 1) * 4 + (t_of >> 1)) * 32 + (rr >> 4) * 2 + (rr & 1))
    hidb[...] = dot(to_b, hidden).astype(BF16)
    for copy in weight_copies[2 * W_PARTS :]:
        copy.wait()

    def down_a(n):
        y = dot(hid[...], wd[:, n * CHUNK : (n + 1) * CHUNK])
        pa[n] = y.astype(BF16).reshape(2, 128, CHUNK)
        pm[n] = jnp.where(core == 0, y[:128], y[128:])
        remote(pa.at[n, 1 - core], cr.at[n], rcs.at[n], rcr.at[n], other_dev).start()

    def chip_sum(n):
        remote(pa.at[n, 1 - core], cr.at[n], rcs.at[n], rcr.at[n], other_dev).wait_recv()
        both = pm[n] + cr[n].astype(F32)
        pm[n] = both
        cs[n] = both.astype(BF16).reshape(4, 32, CHUNK)
        for copy in ret_far(n):
            copy.start()

    def ret_far(n):
        a = remote(
            cs.at[n, opposite, pl.ds(0, 16), :], far.at[0, n], rfs.at[0, n], rfr.at[0, n], right_dev
        )
        b = remote(
            cs.at[n, opposite, pl.ds(16, 16), :], far.at[1, n], rfs.at[1, n], rfr.at[1, n], left_dev
        )
        return a, b

    def ret_near(n):
        a = remote(cs.at[n, right], near.at[0, n], rns.at[0, n], rnr.at[0, n], right_dev)
        b = remote(cs.at[n, left], near.at[1, n], rns.at[1, n], rnr.at[1, n], left_dev)
        return a, b

    def ret_relay(n):
        for copy in ret_far(n):
            copy.wait_recv()
        to_right = pl.ds(pl.multiple_of(right * 32, 32), 16)
        to_left = pl.ds(pl.multiple_of(left * 32 + 16, 16), 16)
        cs[n, right, 0:16, :] = (pm[n, to_right, :] + far[0, n].astype(F32)).astype(BF16)
        cs[n, left, 16:32, :] = (pm[n, to_left, :] + far[1, n].astype(F32)).astype(BF16)
        for copy in ret_near(n):
            copy.start()

    def ret_sum(n):
        for copy in ret_near(n):
            copy.wait_recv()
        rows = pl.ds(pl.multiple_of(x * 32, 32), 32)
        y = pm[n, rows, :] + near[0, n].astype(F32) + near[1, n].astype(F32)
        y = y.astype(BF16)
        for p in range(2):
            y2[(n * 2 + p) * 32 : (n * 2 + p) * 32 + 32, :] = y[:, p * 512 : p * 512 + 512]

    def b_core():
        return remote(pbs, cbr, rbcs, rbcr, other_dev)

    down_a(0)
    b0 = dot(hidb[...], wd[:, A_COLS : A_COLS + CHUNK])
    b1 = dot(hidb[...], wd[:, A_COLS + CHUNK : A_COLS + 2 * CHUNK])
    pbs[...] = jnp.where(core == 0, b1, b0).astype(BF16)
    pbm[...] = jnp.where(core == 0, b0, b1)
    b_core().start()
    chip_sum(0)
    down_a(1)
    b_core().wait_recv()
    bsend[...] = (pbm[...] + cbr[...].astype(F32)).astype(BF16).reshape(16, 16, CHUNK)
    bback[me] = bsend[me]

    def send_b3(step, carry):
        peer, device = plane(step)
        remote(bsend.at[peer], bback.at[me], rbs.at[step], rbr.at[me], device).start()
        return carry

    lax.fori_loop(1, 16, send_b3, 0)
    ret_relay(0)
    chip_sum(1)
    down_a(2)
    ret_relay(1)
    chip_sum(2)
    down_a(3)
    ret_sum(0)
    ret_relay(2)
    chip_sum(3)
    ret_sum(1)
    ret_relay(3)

    rr = iota((128, 256), 0)
    ll = iota((128, 256), 1)
    wide_hi = dot_nt(dot(wide, whi).astype(BF16), spread_b)
    wide_lo = dot_nt(dot(wide, wlo).astype(BF16), spread_b)

    def wait_b3(step, carry):
        peer, device = plane(step)
        remote(bsend.at[peer], bback.at[peer], rbs.at[step], rbr.at[peer], device).wait_recv()
        return carry

    lax.fori_loop(1, 16, wait_b3, 0)
    partial = jnp.zeros((128, 256), F32)
    for q in range(4):
        keep = ((rr >> 4) == ((ll & 15) >> 1)) & (((rr & 15) >> 2) == q)
        piece = bback[:, :, q * 256 : q * 256 + 256].reshape(256, 256)
        partial = partial + dot(jnp.where(keep, wide_hi, 0.0).astype(BF16), piece)
        partial = partial + dot(jnp.where(keep, wide_lo, 0.0).astype(BF16), piece)
    fsend[...] = partial.astype(BF16).reshape(8, 16, 256)
    frecv[tp] = fsend[tp]

    def send_b4(step, carry):
        peer, device = column(step)
        remote(fsend.at[peer], frecv.at[tp], rfis.at[step], rfir.at[tp], device).start()
        return carry

    lax.fori_loop(1, 8, send_b4, 0)
    ret_sum(2)
    ret_sum(3)
    rr = iota((256, 256), 0)
    ll = iota((256, 256), 1)
    repack_a = onehot(ll == (rr & 7) * 32 + (rr >> 3))
    asend[...] = dot(repack_a, y2[...]).astype(BF16).reshape(16, 16, 512)
    aback[me] = asend[me]

    def send_a2(step, carry):
        peer, device = plane(step)
        remote(asend.at[peer], aback.at[me], ras.at[step], rar.at[me], device).start()
        return carry

    lax.fori_loop(1, 16, send_a2, 0)

    def wait_b4(step, carry):
        peer, device = column(step)
        remote(fsend.at[peer], frecv.at[peer], rfis.at[step], rfir.at[peer], device).wait_recv()
        return carry

    lax.fori_loop(1, 8, wait_b4, 0)
    rr = iota((64, 128), 0)
    ll = iota((64, 128), 1)
    gather = onehot(
        ((rr >> 5) == ((ll >> 4) & 1))
        & (((rr >> 3) & 3) == ((ll & 15) >> 2))
        & ((rr & 7) == (ll & 3))
    )
    home_b = dot(gather, frecv[...].reshape(128, 256))
    for piece in range(8):
        start = A_COLS + piece * 256
        out[:, start : start + 256] = (
            stream[0:4, start : start + 256] + home_b[piece * 8 : piece * 8 + 4, :]
        ).astype(BF16)

    rr = iota((64, 256), 0)
    ll = iota((64, 256), 1)
    keep = (rr >> 3) == (ll & 7)
    home_hi = dot_nt(dot(mine[0:64], whi).astype(BF16), spread_a)
    home_lo = dot_nt(dot(mine[0:64], wlo).astype(BF16), spread_a)
    home_hi = jnp.where(keep, home_hi, 0.0).astype(BF16)
    home_lo = jnp.where(keep, home_lo, 0.0).astype(BF16)

    def wait_a2(step, carry):
        peer, device = plane(step)
        remote(asend.at[peer], aback.at[peer], ras.at[step], rar.at[peer], device).wait_recv()
        return carry

    lax.fori_loop(1, 16, wait_a2, 0)
    back = aback[...].reshape(256, 512)
    home_a = dot(home_hi, back) + dot(home_lo, back)
    for p in range(8):
        cols = slice(p * 512, p * 512 + 512)
        out[:, cols] = (stream[0:4, cols] + home_a[p * 8 : p * 8 + 4, :]).astype(BF16)

    def drain_plane(step, carry):
        peer, device = plane(step)
        remote(apack.at[peer], arecv.at[me], a1s.at[step], a1r.at[me], device).wait_send()
        remote(bpack.at[peer], xbh.at[core, me], b2s.at[step], b2r.at[me], device).wait_send()
        remote(bsend.at[peer], bback.at[me], rbs.at[step], rbr.at[me], device).wait_send()
        remote(asend.at[peer], aback.at[me], ras.at[step], rar.at[me], device).wait_send()
        return carry

    lax.fori_loop(1, 16, drain_plane, 0)

    def drain_column(step, carry):
        peer, device = column(step)
        remote(bmsg, xb1.at[tp], b1s.at[step], b1r.at[tp], device).wait_send()
        remote(fsend.at[peer], frecv.at[tp], rfis.at[step], rfir.at[tp], device).wait_send()
        return carry

    lax.fori_loop(1, 8, drain_column, 0)
    bcore.wait_send()
    b_core().wait_send()
    for n in range(A_CHUNKS):
        for copy in (*near_in(n), *far_sends(n), *ret_far(n), *ret_near(n), core_send(n)):
            copy.wait_send()
        remote(pa.at[n, 1 - core], cr.at[n], rcs.at[n], rcr.at[n], other_dev).wait_send()


def layer(
    resid,
    query,
    key_cache,
    value_cache,
    new_key,
    new_value,
    cache_len,
    norm_gain,
    routes,
    gate_fixed,
    w_gate,
    w_up,
    w_down,
):
    vmem = pl.BlockSpec(memory_space=pltpu.VMEM)
    anywhere = pl.BlockSpec(memory_space=pl.ANY)
    dma = pltpu.SemaphoreType.DMA
    n = A_CHUNKS
    scratch = [
        pltpu.VMEM((ROWS, LENGTH, 1024), BF16),
        pltpu.VMEM((ROWS, LENGTH, 1024), BF16),
        pltpu.VMEM((HIDDEN, D), BF16),
        pltpu.VMEM((HIDDEN, D), BF16),
        pltpu.VMEM((HIDDEN, D), BF16),
        pltpu.VMEM((HEADS * ROWS, 128), F32),
        pltpu.VMEM((HEADS * ROWS, 128), F32),
        pltpu.VMEM((GROUP * ROWS, 1024), F32),
        pltpu.VMEM((GROUP * ROWS, 1024), F32),
        pltpu.VMEM((HEADS * ROWS, 128), F32),
        pltpu.VMEM((8, D), F32),
        pltpu.VMEM((96, 512), F32),
        pltpu.VMEM((16, 16, 512), BF16),
        pltpu.VMEM((16, 16, 512), BF16),
        pltpu.VMEM((16, 512), BF16),
        pltpu.VMEM((8, 16, 512), BF16),
        pltpu.VMEM((16, 16, CHUNK), BF16),
        pltpu.VMEM((2, 16, 16, CHUNK), BF16),
        pltpu.VMEM((n, 2, 4, 32, CHUNK), BF16),
        pltpu.VMEM((256, HIDDEN), F32),
        pltpu.VMEM((256, HIDDEN), F32),
        pltpu.VMEM((256, HIDDEN), BF16),
        pltpu.VMEM((256, HIDDEN), BF16),
        pltpu.VMEM((n, 2, 128, CHUNK), BF16),
        pltpu.VMEM((n, 128, CHUNK), F32),
        pltpu.VMEM((n, 128, CHUNK), BF16),
        pltpu.VMEM((n, 4, 32, CHUNK), BF16),
        pltpu.VMEM((2, n, 16, CHUNK), BF16),
        pltpu.VMEM((2, n, 32, CHUNK), BF16),
        pltpu.VMEM((256, 512), BF16),
        pltpu.VMEM((16, 16, 512), BF16),
        pltpu.VMEM((16, 16, 512), BF16),
        pltpu.VMEM((256, CHUNK), BF16),
        pltpu.VMEM((256, CHUNK), F32),
        pltpu.VMEM((256, CHUNK), BF16),
        pltpu.VMEM((16, 16, CHUNK), BF16),
        pltpu.VMEM((16, 16, CHUNK), BF16),
        pltpu.VMEM((8, 16, 256), BF16),
        pltpu.VMEM((8, 16, 256), BF16),
        dma((2 + 3 * W_PARTS,)),
        dma((16,)),
        dma((16,)),
        dma((8,)),
        dma((8,)),
        dma((16,)),
        dma((16,)),
        dma,
        dma,
        dma((2, n)),
        dma((2, n)),
        dma((2, n)),
        dma((2, n)),
        dma((n,)),
        dma((n,)),
        dma((n,)),
        dma((n,)),
        dma((2, n)),
        dma((2, n)),
        dma((2, n)),
        dma((2, n)),
        dma((16,)),
        dma((16,)),
        dma,
        dma,
        dma((16,)),
        dma((16,)),
        dma((8,)),
        dma((8,)),
    ]
    return pl.pallas_call(
        kernel,
        out_shape=jax.ShapeDtypeStruct((ROWS, D), BF16),
        in_specs=[pl.BlockSpec(memory_space=pltpu.SMEM)] + [vmem] * 7 + [anywhere] * 5,
        out_specs=vmem,
        scratch_shapes=scratch,
        compiler_params=pltpu.CompilerParams(
            collective_id=0, has_side_effects=True, vmem_limit_bytes=60 * 1024 * 1024
        ),
        cost_estimate=pl.CostEstimate(
            flops=2 * 3 * 256 * HIDDEN * D, bytes_accessed=27 * 1024 * 1024, transcendentals=0
        ),
    )(
        cache_len,
        resid,
        query,
        new_key,
        new_value,
        norm_gain.reshape(1, D),
        routes,
        gate_fixed,
        key_cache,
        value_cache,
        w_gate,
        w_up,
        w_down,
    )


def solution(mesh):
    placed = (
        P(("side", "expert", "tp"), None),
        P(("side", "expert", "tp"), None),
        P(("side", "expert", "tp"), None, None),
        P(("side", "expert", "tp"), None, None),
        P(("side", "expert", "tp"), None),
        P(("side", "expert", "tp"), None),
        P(("side", "expert", "tp")),
        P(),
        P(("side", "expert"), None),
        P(("side", "expert"), None),
        P(("side", "expert"), "tp", None),
        P(("side", "expert"), "tp", None),
        P(("side", "expert"), "tp", None),
    )
    return jax.shard_map(
        layer,
        mesh=mesh,
        in_specs=placed,
        out_specs=P(("side", "expert", "tp"), None),
        check_vma=False,
    )
```

time: 152 us -> 70.3 us (0.46)
  Pallas kernels: 0 us -> 65.9 us
  blocking collectives: 52.7 us -> 0 us
  waiting for transfers between devices: 40.7 us -> 0 us
  matrix products: 23.4 us -> 0 us
  local copies, waits for them, and re-layouts: 18.1 us -> 4.16 us
  other arithmetic: 9.34 us -> 0 us
  starting transfers between devices: 6.08 us -> 0 us
    pallas_call x0 -> x1, Pallas kernels: none -> 65.9 us  [layer(): pl.pallas_call(kernel, out_shape=jax.ShapeDtypeStruct((ROWS, D), BF16), i...]
    all_to_all x1 -> x0, blocking collectives: 52.7 us -> none  [shards(): lax.all_to_all(outgoing, ('side', 'expert', 'tp'), split_axis=0, concat_a...]
    all_to_all x1 -> x0, waiting for transfers between devices: 40.7 us -> none  [shards(): lax.all_to_all(partial_out.astype(jnp.bfloat16), ('side', 'expert', 'tp')...]
    dot_general x8 -> x0, matrix products: 23.4 us -> none  [the longest x1 6.77 us: expert_ffn(): lax.dot_general(flat, w_gate[0], dims, preferred_element_type=jnp.float32)]
    reshape x5 -> x0, local copies, waits for them, and re-layouts: 9.49 us -> none  [the longest x1 7.33 us: expert_ffn(): flat = arrived.reshape(-1, arrived.shape[-1])]
    reduce_sum x7 -> x0, other arithmetic: 7.57 us -> none  [the longest x1 5.05 us: shards(): summed = jnp.sum(returned.reshape(experts, slices, capacity, D), axis=1)]
    all_to_all x1 -> x0, starting transfers between devices: 6.08 us -> none  [shards(): lax.all_to_all(partial_out.astype(jnp.bfloat16), ('side', 'expert', 'tp')...]
    convert_element_type x2 -> x0, local copies, waits for them, and re-layouts: 5.11 us -> none  [the longest x1 4.94 us: shards(): partial_out.astype(jnp.bfloat16)]
  transfers between devices with their start and end apart: 1 -> 0, of which waited for: 1 -> 0; matrix products, arithmetic and copies ran while one was open for 0% -> 0% of each run, Pallas kernels for 0% -> 0%
where the time goes in v1:
time: 70.3 us; the launch traced here: 70.1 us
  Pallas kernels  65.9 us (94%)
  local copies, waits for them, and re-layouts  4.16 us (6%)
    pallas_call x1, Pallas kernels, layer(): pl.pallas_call(kernel, out_shape=jax.ShapeDtypeStruct((ROWS, D), BF16), i...  65.9 us
    unnamed x3, local copies, waits for them, and re-layouts  4.16 us

profile of v1, /device:TPU:0, one launch (start us, length us, event | category | flops | bytes accessed | tf_op | source)
XLA Modules:
  0.0 70.1 jit_solution(10970486167639140379)
XLA Ops:
  0.0 1.4 %copy.14.routes = s32[32,4]{1,0:T(8,128)} copy(s32[32,4]{0,1:T(4,128)} %param.21) | data formatting | bytes 1024 | tf_op args[8]
  1.4 1.4 %copy.15.gates = s32[32,4]{1,0:T(8,128)} copy(s32[32,4]{0,1:T(4,128)} %param.22) | data formatting | bytes 1024 | tf_op args[9]
  2.7 65.9 %shard_map.127 = bf16[4,6144]{1,0:T(4,128)(2,1)} custom-call(s32[4]{0:T(128)} %clen.1, bf16[4,6144]{1,0:T(4,128)(2,1)} %resid.1, bf16[4,6144]{1,0:T(4,128)(2,1)} %query.1, bf16[4,1024]{1,0:T(4,128)(2,1)} %new_key.1, bf16[4,1024]{1,0:T(4,128)(2,1)} %new_value.1, f32[1,6144]{1,0:T(1,128)} %bitcast.1, s32[32,4]{1,0:T(8,128)} %copy.14.routes, ...), custom_call_target="tpu_custom_call" | custom-call | flops 6341787648 | bytes 28311552 | tf_op jit(solution)/shard_map/pallas_call | solution.py:736
  68.6 1.4 %copy.17 = bf16[4,6144]{1,0:T(4,128)(2,1)} copy(bf16[4,6144]{1,0:T(4,128)(2,1)} %shard_map.127) | data formatting | bytes 98304

commit v2 on v1

--- a/solution.py
+++ b/solution.py
@@ -23,6 +23,7 @@
 MESH = pl.DeviceIdType.MESH
 W_PARTS = 3
 W_ROWS = HIDDEN // W_PARTS
+PLANE = ((1, 0), (0, 1), (3, 0), (0, 3), (1, 1), (3, 3), (1, 3), (3, 1), (2, 0), (0, 2), (2, 1), (1, 2), (2, 3), (3, 2), (2, 2))
 
 
 def iota(shape, dim):
@@ -161,6 +162,10 @@
         peer = lax.rem(tp + step, 8)
         return peer, (side, expert, peer)
 
+    def whole(buffer, count, send_sem, recv_sem):
+        part = buffer.at[pl.ds(0, count)]
+        return remote(part, part, send_sem, recv_sem, other_dev)
+
     barrier = pltpu.get_barrier_semaphore()
 
     def greet_plane(step, carry):
@@ -183,7 +188,7 @@
                 pltpu.make_async_copy(
                     src.at[0, rows, :],
                     dst.at[rows, :],
-                    local_sem.at[2 + number * W_PARTS + part],
+                    local_sem.at[2 + number],
                 )
             )
     for copy in weight_copies:
@@ -213,17 +218,17 @@
     lane32 = iota((32, 32), 1)
     row32 = iota((32, 32), 0)
     fixed = gates[...].astype(F32)
-    weights = fixed / jnp.sum(fixed, axis=-1, keepdims=True)
+    weights = fixed / jnp.sum(fixed, axis=0, keepdims=True)
     chosen = jnp.zeros((32, 32), F32)
     weighted = jnp.zeros((32, 32), F32)
     route = routes[...]
     for k in range(4):
-        same = route[:, k : k + 1] == (lane32 >> 1)
+        same = route[k : k + 1, :] == (row32 >> 1)
         chosen = chosen + jnp.where(same, 1.0, 0.0)
-        weighted = weighted + jnp.where(same, weights[:, k : k + 1], 0.0)
-    earlier = onehot(((row32 >> 2) == (lane32 >> 2)) & (lane32 < row32))
-    before = dot(earlier, chosen.astype(BF16))
-    picked = (chosen > 0.5) & (jnp.abs(before - (lane32 & 1).astype(F32)) < 0.5)
+        weighted = weighted + jnp.where(same, weights[k : k + 1, :], 0.0)
+    earlier = onehot(((row32 >> 2) == (lane32 >> 2)) & (row32 < lane32))
+    before = dot(chosen.astype(BF16), earlier)
+    picked = (chosen > 0.5) & (jnp.abs(before - (row32 & 1).astype(F32)) < 0.5)
     sel = onehot(picked)
     wsel = jnp.where(picked, weighted, 0.0)
     whi = wsel.astype(BF16)
@@ -239,14 +244,14 @@
     rr = iota((128, 32), 0)
     ll = iota((128, 32), 1)
     wide = onehot(ll == ((rr >> 4) * 4 + (rr & 3)))
-    pack_a = dot_nt(spread_a, dot(mine, sel).astype(BF16))
+    pack_a = dot_nt(spread_a, dot_nt(mine, sel).astype(BF16))
     rr = iota((256, 96), 0)
     ll = iota((256, 96), 1)
     pack_a = jnp.where((rr & 7) == (ll >> 3), pack_a, 0.0).astype(BF16)
     rr = iota((16, 96), 0)
     ll = iota((16, 96), 1)
     pack_b1 = onehot(ll == (8 + (rr >> 2)) * 8 + (rr & 3))
-    pack_b = dot_nt(spread_b, dot(wide, sel).astype(BF16))
+    pack_b = dot_nt(spread_b, dot_nt(wide, sel).astype(BF16))
     rr = iota((256, 128), 0)
     ll = iota((256, 128), 1)
     pack_b = jnp.where(((rr & 15) >> 1) == (ll >> 4), pack_b, 0.0)
@@ -304,7 +309,7 @@
 
     def send_b1(step, carry):
         peer, device = column(step)
-        remote(bmsg, xb1.at[tp], b1s.at[step], b1r.at[tp], device).start()
+        remote(bmsg, xb1.at[tp], b1s, b1r, device).start()
         return carry
 
     lax.fori_loop(1, 8, send_b1, 0)
@@ -312,19 +317,12 @@
     apack[...] = packed.reshape(16, 16, 512)
     arecv[me] = apack[me]
 
-    def send_a1(step, carry):
+    for dy, dz in PLANE:
+        step = dy * 4 + dz
         peer, device = plane(step)
-        remote(apack.at[peer], arecv.at[me], a1s.at[step], a1r.at[me], device).start()
-        return carry
-
-    lax.fori_loop(1, 16, send_a1, 0)
-
-    def wait_b1(step, carry):
-        peer, device = column(step)
-        remote(bmsg, xb1.at[peer], b1s.at[step], b1r.at[peer], device).wait_recv()
-        return carry
-
-    lax.fori_loop(1, 8, wait_b1, 0)
+        remote(apack.at[peer], arecv.at[me], a1s, a1r, device).start()
+
+    whole(xb1, 7, b1s, b1r).wait_recv()
     xb_all = xb1[...].reshape(128, 512)
     for i in range(2):
         pick = jnp.where(((ll & 15) >> 2) == core * 2 + i, pack_b, 0.0).astype(BF16)
@@ -333,19 +331,12 @@
         )
     xbh[core, me] = bpack[me]
 
-    def send_b2(step, carry):
+    for dy, dz in PLANE:
+        step = dy * 4 + dz
         peer, device = plane(step)
-        remote(bpack.at[peer], xbh.at[core, me], b2s.at[step], b2r.at[me], device).start()
-        return carry
-
-    lax.fori_loop(1, 16, send_b2, 0)
-
-    def wait_a1(step, carry):
-        peer, device = plane(step)
-        remote(apack.at[peer], arecv.at[peer], a1s.at[step], a1r.at[peer], device).wait_recv()
-        return carry
-
-    lax.fori_loop(1, 16, wait_a1, 0)
+        remote(bpack.at[peer], xbh.at[core, me], b2s, b2r, device).start()
+
+    whole(arecv, 15, a1s, a1r).wait_recv()
     rr = iota((256, 256), 0)
     ll = iota((256, 256), 1)
     unpack_a = onehot(ll == (rr & 31) * 8 + (rr >> 5))
@@ -355,38 +346,38 @@
 
     def near_in(n):
         mine_ref = xa.at[n, core, x]
-        to_right = remote(mine_ref, mine_ref, ns.at[0, n], nr.at[0, n], right_dev)
-        to_left = remote(mine_ref, mine_ref, ns.at[1, n], nr.at[1, n], left_dev)
+        to_right = remote(mine_ref, mine_ref, ns, nr.at[0, n], right_dev)
+        to_left = remote(mine_ref, mine_ref, ns, nr.at[1, n], left_dev)
         return to_right, to_left
 
     def near_arrivals(n):
         from_left = xa.at[n, core, left]
         from_right = xa.at[n, core, right]
-        a = remote(from_left, from_left, ns.at[0, n], nr.at[0, n], right_dev)
-        b = remote(from_right, from_right, ns.at[1, n], nr.at[1, n], left_dev)
+        a = remote(from_left, from_left, ns, nr.at[0, n], right_dev)
+        b = remote(from_right, from_right, ns, nr.at[1, n], left_dev)
         return a, b
 
     def far_sends(n):
         low = xa.at[n, core, left, pl.ds(0, 16), :]
         high = xa.at[n, core, right, pl.ds(16, 16), :]
-        a = remote(low, low, fs.at[0, n], fr.at[0, n], right_dev)
-        b = remote(high, high, fs.at[1, n], fr.at[1, n], left_dev)
+        a = remote(low, low, fs, fr.at[0, n], right_dev)
+        b = remote(high, high, fs, fr.at[1, n], left_dev)
         return a, b
 
     def far_arrivals(n):
         low = xa.at[n, core, opposite, pl.ds(0, 16), :]
         high = xa.at[n, core, opposite, pl.ds(16, 16), :]
-        a = remote(low, low, fs.at[0, n], fr.at[0, n], right_dev)
-        b = remote(high, high, fs.at[1, n], fr.at[1, n], left_dev)
+        a = remote(low, low, fs, fr.at[0, n], right_dev)
+        b = remote(high, high, fs, fr.at[1, n], left_dev)
         return a, b
 
     def core_send(n):
         half = xa.at[n, core]
-        return remote(half, half, acs.at[n], acr.at[n], other_dev)
+        return remote(half, half, acs, acr.at[n], other_dev)
 
     def core_arrival(n):
         half = xa.at[n, 1 - core]
-        return remote(half, half, acs.at[n], acr.at[n], other_dev)
+        return remote(half, half, acs, acr.at[n], other_dev)
 
     for n in range(A_CHUNKS):
         for copy in near_in(n):
@@ -394,8 +385,8 @@
 
     accg[...] = jnp.zeros((256, HIDDEN), F32)
     accu[...] = jnp.zeros((256, HIDDEN), F32)
-    for copy in weight_copies[: 2 * W_PARTS]:
-        copy.wait()
+    pltpu.make_async_copy(wg_hbm.at[0], wg, local_sem.at[2]).wait()
+    pltpu.make_async_copy(wu_hbm.at[0], wu, local_sem.at[3]).wait()
 
     def project(value, offset):
         cols = pl.ds(offset, CHUNK)
@@ -417,36 +408,30 @@
             copy.wait_recv()
         core_send(n).start()
 
-    relay(0)
-    relay(1)
+    for n in range(A_CHUNKS):
+        relay(n)
     forward(0)
-    relay(2)
-    forward(1)
-    project_a(0)
-
-    def wait_b2(step, carry):
-        peer, device = plane(step)
-        remote(
-            bpack.at[peer], xbh.at[core, peer], b2s.at[step], b2r.at[peer], device
-        ).wait_recv()
-        return carry
-
-    lax.fori_loop(1, 16, wait_b2, 0)
+
+    whole(xbh.at[core], 15, b2s, b2r).wait_recv()
     bcore = remote(xbh.at[core], xbh.at[core], bcs, bcr, other_dev)
     bcore.start()
-    relay(3)
+    forward(1)
+    tau = rr >> 5
+    unpack_b = onehot(
+        ll == ((rr & 31) >> 1) * 16 + ((tau & 3) * 2 + (tau >> 2)) * 2 + (rr & 1)
+    )
+
+    def project_b(half):
+        offset = pl.multiple_of(A_COLS + half * CHUNK, CHUNK)
+        project(dot(unpack_b, xbh[half].reshape(256, CHUNK)).astype(BF16), offset)
+
+    project_a(0)
+    project_b(core)
     forward(2)
     project_a(1)
     forward(3)
     remote(xbh.at[1 - core], xbh.at[1 - core], bcs, bcr, other_dev).wait_recv()
-    tau = rr >> 5
-    unpack_b = onehot(
-        ll == ((rr & 31) >> 1) * 16 + ((tau & 3) * 2 + (tau >> 2)) * 2 + (rr & 1)
-    )
-    for h in range(2):
-        project(
-            dot(unpack_b, xbh[h].reshape(256, CHUNK)).astype(BF16), A_COLS + h * CHUNK
-        )
+    project_b(1 - core)
     project_a(2)
     project_a(3)
     g = accg[...]
@@ -455,17 +440,31 @@
     t_of = (rr & 15) >> 1
     to_b = onehot(ll == ((t_of & 1) * 4 + (t_of >> 1)) * 32 + (rr >> 4) * 2 + (rr & 1))
     hidb[...] = dot(to_b, hidden).astype(BF16)
-    for copy in weight_copies[2 * W_PARTS :]:
-        copy.wait()
+    pltpu.make_async_copy(wd_hbm.at[0], wd, local_sem.at[4]).wait()
+
+    def drain():
+        whole(xb1, 7, b1s, b1r).wait_send()
+        whole(arecv, 15, a1s, a1r).wait_send()
+        whole(xbh.at[core], 15, b2s, b2r).wait_send()
+        bcore.wait_send()
+        remote(xa.at[0], xa.at[0], ns, nr.at[0, 0], other_dev).wait_send()
+        remote(xa.at[0, 0], xa.at[0, 0], fs, fr.at[0, 0], other_dev).wait_send()
+        remote(xa.at[0:2], xa.at[0:2], acs, acr.at[0], other_dev).wait_send()
+        remote(cr, cr, rcs, rcr.at[0], other_dev).wait_send()
+        b_core().wait_send()
+        whole(bback, 15, rbs, rbr).wait_send()
+        remote(far, far, rfs, rfr.at[0, 0], other_dev).wait_send()
+        remote(near, near, rns, rnr.at[0, 0], other_dev).wait_send()
+        whole(frecv, 7, rfis, rfir).wait_send()
 
     def down_a(n):
         y = dot(hid[...], wd[:, n * CHUNK : (n + 1) * CHUNK])
         pa[n] = y.astype(BF16).reshape(2, 128, CHUNK)
         pm[n] = jnp.where(core == 0, y[:128], y[128:])
-        remote(pa.at[n, 1 - core], cr.at[n], rcs.at[n], rcr.at[n], other_dev).start()
+        remote(pa.at[n, 1 - core], cr.at[n], rcs, rcr.at[n], other_dev).start()
 
     def chip_sum(n):
-        remote(pa.at[n, 1 - core], cr.at[n], rcs.at[n], rcr.at[n], other_dev).wait_recv()
+        remote(pa.at[n, 1 - core], cr.at[n], rcs, rcr.at[n], other_dev).wait_recv()
         both = pm[n] + cr[n].astype(F32)
         pm[n] = both
         cs[n] = both.astype(BF16).reshape(4, 32, CHUNK)
@@ -474,16 +473,16 @@
 
     def ret_far(n):
         a = remote(
-            cs.at[n, opposite, pl.ds(0, 16), :], far.at[0, n], rfs.at[0, n], rfr.at[0, n], right_dev
+            cs.at[n, opposite, pl.ds(0, 16), :], far.at[0, n], rfs, rfr.at[0, n], right_dev
         )
         b = remote(
-            cs.at[n, opposite, pl.ds(16, 16), :], far.at[1, n], rfs.at[1, n], rfr.at[1, n], left_dev
+            cs.at[n, opposite, pl.ds(16, 16), :], far.at[1, n], rfs, rfr.at[1, n], left_dev
         )
         return a, b
 
     def ret_near(n):
-        a = remote(cs.at[n, right], near.at[0, n], rns.at[0, n], rnr.at[0, n], right_dev)
-        b = remote(cs.at[n, left], near.at[1, n], rns.at[1, n], rnr.at[1, n], left_dev)
+        a = remote(cs.at[n, right], near.at[0, n], rns, rnr.at[0, n], right_dev)
+        b = remote(cs.at[n, left], near.at[1, n], rns, rnr.at[1, n], left_dev)
         return a, b
 
     def ret_relay(n):
@@ -508,47 +507,46 @@
     def b_core():
         return remote(pbs, cbr, rbcs, rbcr, other_dev)
 
-    down_a(0)
     b0 = dot(hidb[...], wd[:, A_COLS : A_COLS + CHUNK])
     b1 = dot(hidb[...], wd[:, A_COLS + CHUNK : A_COLS + 2 * CHUNK])
     pbs[...] = jnp.where(core == 0, b1, b0).astype(BF16)
     pbm[...] = jnp.where(core == 0, b0, b1)
     b_core().start()
+    down_a(0)
+    down_a(1)
     chip_sum(0)
-    down_a(1)
     b_core().wait_recv()
     bsend[...] = (pbm[...] + cbr[...].astype(F32)).astype(BF16).reshape(16, 16, CHUNK)
     bback[me] = bsend[me]
-
-    def send_b3(step, carry):
+    for dy, dz in PLANE:
+        step = dy * 4 + dz
         peer, device = plane(step)
-        remote(bsend.at[peer], bback.at[me], rbs.at[step], rbr.at[me], device).start()
-        return carry
-
-    lax.fori_loop(1, 16, send_b3, 0)
-    ret_relay(0)
+        remote(bsend.at[peer], bback.at[me], rbs, rbr, device).start()
+    down_a(2)
     chip_sum(1)
-    down_a(2)
-    ret_relay(1)
+    down_a(3)
     chip_sum(2)
-    down_a(3)
-    ret_sum(0)
-    ret_relay(2)
     chip_sum(3)
-    ret_sum(1)
-    ret_relay(3)
+    for n in range(A_CHUNKS):
+        ret_relay(n)
+    for n in range(A_CHUNKS):
+        ret_sum(n)
+    rr = iota((256, 256), 0)
+    ll = iota((256, 256), 1)
+    repack_a = onehot(ll == (rr & 7) * 32 + (rr >> 3))
+    asend[...] = dot(repack_a, y2[...]).astype(BF16).reshape(16, 16, 512)
+    aback[me] = asend[me]
+    for dy, dz in PLANE:
+        step = dy * 4 + dz
+        peer, device = plane(step)
+        remote(asend.at[peer], aback.at[me], ras, rar, device).start()
 
     rr = iota((128, 256), 0)
     ll = iota((128, 256), 1)
-    wide_hi = dot_nt(dot(wide, whi).astype(BF16), spread_b)
-    wide_lo = dot_nt(dot(wide, wlo).astype(BF16), spread_b)
-
-    def wait_b3(step, carry):
-        peer, device = plane(step)
-        remote(bsend.at[peer], bback.at[peer], rbs.at[step], rbr.at[peer], device).wait_recv()
-        return carry
-
-    lax.fori_loop(1, 16, wait_b3, 0)
+    wide_hi = dot_nt(dot_nt(wide, whi).astype(BF16), spread_b)
+    wide_lo = dot_nt(dot_nt(wide, wlo).astype(BF16), spread_b)
+
+    whole(bback, 15, rbs, rbr).wait_recv()
     partial = jnp.zeros((128, 256), F32)
     for q in range(4):
         keep = ((rr >> 4) == ((ll & 15) >> 1)) & (((rr & 15) >> 2) == q)
@@ -560,31 +558,11 @@
 
     def send_b4(step, carry):
         peer, device = column(step)
-        remote(fsend.at[peer], frecv.at[tp], rfis.at[step], rfir.at[tp], device).start()
+        remote(fsend.at[peer], frecv.at[tp], rfis, rfir, device).start()
         return carry
 
     lax.fori_loop(1, 8, send_b4, 0)
-    ret_sum(2)
-    ret_sum(3)
-    rr = iota((256, 256), 0)
-    ll = iota((256, 256), 1)
-    repack_a = onehot(ll == (rr & 7) * 32 + (rr >> 3))
-    asend[...] = dot(repack_a, y2[...]).astype(BF16).reshape(16, 16, 512)
-    aback[me] = asend[me]
-
-    def send_a2(step, carry):
-        peer, device = plane(step)
-        remote(asend.at[peer], aback.at[me], ras.at[step], rar.at[me], device).start()
-        return carry
-
-    lax.fori_loop(1, 16, send_a2, 0)
-
-    def wait_b4(step, carry):
-        peer, device = column(step)
-        remote(fsend.at[peer], frecv.at[peer], rfis.at[step], rfir.at[peer], device).wait_recv()
-        return carry
-
-    lax.fori_loop(1, 8, wait_b4, 0)
+    whole(frecv, 7, rfis, rfir).wait_recv()
     rr = iota((64, 128), 0)
     ll = iota((64, 128), 1)
     gather = onehot(
@@ -602,46 +580,20 @@
     rr = iota((64, 256), 0)
     ll = iota((64, 256), 1)
     keep = (rr >> 3) == (ll & 7)
-    home_hi = dot_nt(dot(mine[0:64], whi).astype(BF16), spread_a)
-    home_lo = dot_nt(dot(mine[0:64], wlo).astype(BF16), spread_a)
+    home_hi = dot_nt(dot_nt(mine[0:64], whi).astype(BF16), spread_a)
+    home_lo = dot_nt(dot_nt(mine[0:64], wlo).astype(BF16), spread_a)
     home_hi = jnp.where(keep, home_hi, 0.0).astype(BF16)
     home_lo = jnp.where(keep, home_lo, 0.0).astype(BF16)
 
-    def wait_a2(step, carry):
-        peer, device = plane(step)
-        remote(asend.at[peer], aback.at[peer], ras.at[step], rar.at[peer], device).wait_recv()
-        return carry
-
-    lax.fori_loop(1, 16, wait_a2, 0)
+    drain()
+    whole(aback, 15, ras, rar).wait_recv()
     back = aback[...].reshape(256, 512)
     home_a = dot(home_hi, back) + dot(home_lo, back)
     for p in range(8):
         cols = slice(p * 512, p * 512 + 512)
         out[:, cols] = (stream[0:4, cols] + home_a[p * 8 : p * 8 + 4, :]).astype(BF16)
 
-    def drain_plane(step, carry):
-        peer, device = plane(step)
-        remote(apack.at[peer], arecv.at[me], a1s.at[step], a1r.at[me], device).wait_send()
-        remote(bpack.at[peer], xbh.at[core, me], b2s.at[step], b2r.at[me], device).wait_send()
-        remote(bsend.at[peer], bback.at[me], rbs.at[step], rbr.at[me], device).wait_send()
-        remote(asend.at[peer], aback.at[me], ras.at[step], rar.at[me], device).wait_send()
-        return carry
-
-    lax.fori_loop(1, 16, drain_plane, 0)
-
-    def drain_column(step, carry):
-        peer, device = column(step)
-        remote(bmsg, xb1.at[tp], b1s.at[step], b1r.at[tp], device).wait_send()
-        remote(fsend.at[peer], frecv.at[tp], rfis.at[step], rfir.at[tp], device).wait_send()
-        return carry
-
-    lax.fori_loop(1, 8, drain_column, 0)
-    bcore.wait_send()
-    b_core().wait_send()
-    for n in range(A_CHUNKS):
-        for copy in (*near_in(n), *far_sends(n), *ret_far(n), *ret_near(n), core_send(n)):
-            copy.wait_send()
-        remote(pa.at[n, 1 - core], cr.at[n], rcs.at[n], rcr.at[n], other_dev).wait_send()
+    whole(aback, 15, ras, rar).wait_send()
 
 
 def layer(
@@ -703,35 +655,35 @@
         pltpu.VMEM((16, 16, CHUNK), BF16),
         pltpu.VMEM((8, 16, 256), BF16),
         pltpu.VMEM((8, 16, 256), BF16),
-        dma((2 + 3 * W_PARTS,)),
-        dma((16,)),
-        dma((16,)),
-        dma((8,)),
-        dma((8,)),
-        dma((16,)),
-        dma((16,)),
+        dma((5,)),
+        dma,
+        dma,
+        dma,
+        dma,
+        dma,
+        dma,
+        dma,
         dma,
         dma,
         dma((2, n)),
+        dma,
         dma((2, n)),
+        dma,
+        dma((n,)),
+        dma,
+        dma((n,)),
+        dma,
         dma((2, n)),
+        dma,
         dma((2, n)),
-        dma((n,)),
-        dma((n,)),
-        dma((n,)),
-        dma((n,)),
-        dma((2, n)),
-        dma((2, n)),
-        dma((2, n)),
-        dma((2, n)),
-        dma((16,)),
-        dma((16,)),
-        dma,
-        dma,
-        dma((16,)),
-        dma((16,)),
-        dma((8,)),
-        dma((8,)),
+        dma,
+        dma,
+        dma,
+        dma,
+        dma,
+        dma,
+        dma,
+        dma,
     ]
     return pl.pallas_call(
         kernel,
@@ -752,8 +704,8 @@
         new_key,
         new_value,
         norm_gain.reshape(1, D),
-        routes,
-        gate_fixed,
+        routes.T,
+        gate_fixed.T,
         key_cache,
         value_cache,
         w_gate,

time: 70.3 us -> 56.7 us (0.81)
  Pallas kernels: 65.9 us -> 55.1 us
  local copies, waits for them, and re-layouts: 4.16 us -> 1.44 us
    pallas_call x1, Pallas kernels: 65.9 us -> 55.1 us  [layer(): pl.pallas_call(kernel, out_shape=jax.ShapeDtypeStruct((ROWS, D), BF16), i...]
    unnamed x3 -> x1, local copies, waits for them, and re-layouts: 4.16 us -> 1.44 us
where the time goes in v2:
time: 56.7 us; the launch traced here: 56.5 us
  Pallas kernels  55.1 us (97%)
  local copies, waits for them, and re-layouts  1.44 us (3%)
    pallas_call x1, Pallas kernels, layer(): pl.pallas_call(kernel, out_shape=jax.ShapeDtypeStruct((ROWS, D), BF16), i...  55.1 us
    unnamed x1, local copies, waits for them, and re-layouts  1.44 us

profile of v2, /device:TPU:0, one launch (start us, length us, event | category | flops | bytes accessed | tf_op | source)
XLA Modules:
  0.0 56.5 jit_solution(5952808463978671220)
XLA Ops:
  0.0 55.1 %shard_map.127 = bf16[4,6144]{1,0:T(4,128)(2,1)} custom-call(s32[4]{0:T(128)} %clen.1, bf16[4,6144]{1,0:T(4,128)(2,1)} %resid.1, bf16[4,6144]{1,0:T(4,128)(2,1)} %query.1, bf16[4,1024]{1,0:T(4,128)(2,1)} %new_key.1, bf16[4,1024]{1,0:T(4,128)(2,1)} %new_value.1, f32[1,6144]{1,0:T(1,128)} %bitcast.3, s32[4,32]{1,0:T(4,128)} %bitcast.4, s32[4,32]{1,0:T(4,128)} %bitcast.5, ...), custom_call_target="tpu_custom_call" | custom-call | flops 6341787648 | bytes 28311552 | tf_op jit(solution)/shard_map/pallas_call | solution.py:688
  55.1 1.4 %copy.15 = bf16[4,6144]{1,0:T(4,128)(2,1)} copy(bf16[4,6144]{1,0:T(4,128)(2,1)} %shard_map.127) | data formatting | bytes 98304

commit v3 on v2

--- a/solution.py
+++ b/solution.py
@@ -16,6 +16,10 @@
 LENGTH = 128
 HIDDEN = 672
 CHUNK = 1024
+IN_CHUNKS = 3
+IN_A = IN_CHUNKS * CHUNK
+IN_PARTS = ((0, 1), (1, 2))
+PIECE = (D - IN_A) // 4
 A_CHUNKS = 4
 A_COLS = A_CHUNKS * CHUNK
 F32 = jnp.float32
@@ -54,6 +58,20 @@
 
 
 def kernel(
+    clen_hbm,
+    resid_hbm,
+    query_hbm,
+    new_key_hbm,
+    new_value_hbm,
+    gain_hbm,
+    routes_hbm,
+    gates_hbm,
+    key_hbm,
+    value_hbm,
+    wg_hbm,
+    wu_hbm,
+    wd_hbm,
+    out,
     clen,
     resid,
     query,
@@ -62,12 +80,6 @@
     gain,
     routes,
     gates,
-    key_hbm,
-    value_hbm,
-    wg_hbm,
-    wu_hbm,
-    wd_hbm,
-    out,
     kbuf,
     vbuf,
     wg,
@@ -79,9 +91,13 @@
     own_value,
     heads_out,
     stream,
-    xs,
-    apack,
-    arecv,
+    xsa0,
+    xsa1,
+    xsb,
+    apack0,
+    apack1,
+    arecv0,
+    arecv1,
     bmsg,
     xb1,
     bpack,
@@ -176,10 +192,31 @@
         pl.semaphore_signal(barrier, inc=1, device_id=column(step)[1], device_id_type=MESH)
         return carry
 
+    small_copies = [
+        pltpu.make_async_copy(src, dst, local_sem.at[5 + number])
+        for number, (src, dst) in enumerate(
+            (
+                (query_hbm, query),
+                (new_key_hbm, new_key),
+                (new_value_hbm, new_value),
+                (routes_hbm, routes),
+                (gates_hbm, gates),
+                (clen_hbm, clen),
+                (resid_hbm, resid),
+                (gain_hbm, gain),
+            )
+        )
+    ]
+    for copy in small_copies[:6]:
+        copy.start()
     key_copy = pltpu.make_async_copy(key_hbm, kbuf, local_sem.at[0])
     value_copy = pltpu.make_async_copy(value_hbm, vbuf, local_sem.at[1])
     key_copy.start()
     value_copy.start()
+    for copy in small_copies[6:]:
+        copy.start()
+    lax.fori_loop(1, 16, greet_plane, 0)
+    lax.fori_loop(1, 8, greet_column, 0)
     weight_copies = []
     for number, (src, dst) in enumerate(((wg_hbm, wg), (wu_hbm, wu), (wd_hbm, wd))):
         for part in range(W_PARTS):
@@ -193,9 +230,9 @@
             )
     for copy in weight_copies:
         copy.start()
-    lax.fori_loop(1, 16, greet_plane, 0)
-    lax.fori_loop(1, 8, greet_column, 0)
-
+
+    for copy in small_copies[:3]:
+        copy.wait()
     q32 = query[...].astype(F32)
     for head in range(HEADS):
         qs[head * 4 : head * 4 + 4, :] = q32[:, head * 128 : head * 128 + 128]
@@ -204,17 +241,8 @@
     for copy_no in range(GROUP):
         own_key[copy_no * 4 : copy_no * 4 + 4, :] = nk32
         own_value[copy_no * 4 : copy_no * 4 + 4, :] = nv32
-    block = GROUP * ROWS
-    row_of = iota((block, 128), 0) & 3
-    key_copy.wait()
-    for j in range(KV_HEADS):
-        qj = qs[j * block : (j + 1) * block, :].astype(BF16)
-        total = jnp.zeros((block, 128), F32)
-        for r in range(ROWS):
-            part = dot_nt(qj, kbuf[r, :, j * 128 : (j + 1) * 128])
-            total = jnp.where(row_of == r, part, total)
-        scores[j * block : (j + 1) * block, :] = total
-
+    for copy in small_copies[3:6]:
+        copy.wait()
     lane32 = iota((32, 32), 1)
     row32 = iota((32, 32), 0)
     fixed = gates[...].astype(F32)
@@ -238,23 +266,34 @@
     ll = iota((256, 32), 1)
     spread_a = onehot((rr >> 3) == ll)
     spread_b = onehot(ll == ((rr >> 4) * 2 + (rr & 1)))
-    rr = iota((96, 32), 0)
-    ll = iota((96, 32), 1)
+    rr = iota((64, 32), 0)
+    ll = iota((64, 32), 1)
     mine = onehot((ll == tp * 4 + (rr & 7)) & ((rr & 7) < 4))
     rr = iota((128, 32), 0)
     ll = iota((128, 32), 1)
     wide = onehot(ll == ((rr >> 4) * 4 + (rr & 3)))
     pack_a = dot_nt(spread_a, dot_nt(mine, sel).astype(BF16))
-    rr = iota((256, 96), 0)
-    ll = iota((256, 96), 1)
+    rr = iota((256, 64), 0)
+    ll = iota((256, 64), 1)
     pack_a = jnp.where((rr & 7) == (ll >> 3), pack_a, 0.0).astype(BF16)
-    rr = iota((16, 96), 0)
-    ll = iota((16, 96), 1)
-    pack_b1 = onehot(ll == (8 + (rr >> 2)) * 8 + (rr & 3))
+    rr = iota((16, 32), 0)
+    ll = iota((16, 32), 1)
+    pack_b1 = onehot(ll == (rr >> 2) * 8 + (rr & 3))
     pack_b = dot_nt(spread_b, dot_nt(wide, sel).astype(BF16))
     rr = iota((256, 128), 0)
     ll = iota((256, 128), 1)
     pack_b = jnp.where(((rr & 15) >> 1) == (ll >> 4), pack_b, 0.0)
+
+    block = GROUP * ROWS
+    row_of = iota((block, 128), 0) & 3
+    key_copy.wait()
+    for j in range(KV_HEADS):
+        qj = qs[j * block : (j + 1) * block, :].astype(BF16)
+        total = jnp.zeros((block, 128), F32)
+        for r in range(ROWS):
+            part = dot_nt(qj, kbuf[r, :, j * 128 : (j + 1) * 128])
+            total = jnp.where(row_of == r, part, total)
+        scores[j * block : (j + 1) * block, :] = total
 
     pos = iota((HEADS * ROWS, 128), 1)
     row_all = iota((HEADS * ROWS, 128), 0) & 3
@@ -289,6 +328,8 @@
             pr = jnp.where(row_of == r, pj, 0.0).astype(BF16)
             acc = acc + dot(pr, vbuf[r, :, j * 128 : (j + 1) * 128])
         heads_out[j * block : (j + 1) * block, :] = acc
+    for copy in small_copies[6:]:
+        copy.wait()
     stream[...] = jnp.zeros((8, D), F32)
     for head in range(HEADS):
         cols = slice(head * 128, head * 128 + 128)
@@ -298,11 +339,16 @@
     centred = st - mean
     variance = jnp.sum(centred * centred, axis=-1, keepdims=True) * (1.0 / D)
     normed = centred * lax.rsqrt(variance + 1e-05) * gain[...]
-    for p in range(12):
-        xs[p * 8 : p * 8 + 8, :] = normed[:, p * 512 : (p + 1) * 512]
-    xbf = xs[...].astype(BF16)
-
-    bm = dot(pack_b1, xbf).astype(BF16)
+    for xs, (first, chunks) in zip((xsa0, xsa1), IN_PARTS):
+        width = chunks * CHUNK // 8
+        for p in range(8):
+            start = first * CHUNK + p * width
+            xs[p * 8 : p * 8 + 8, :] = normed[:, start : start + width]
+    for p in range(4):
+        start = IN_A + p * PIECE
+        xsb[p * 8 : p * 8 + 8, :] = normed[:, start : start + PIECE]
+
+    bm = dot(pack_b1, xsb[...].astype(BF16)).astype(BF16)
     bmsg[...] = bm
     xb1[tp] = bm
     pl.semaphore_wait(barrier, 22)
@@ -313,36 +359,27 @@
         return carry
 
     lax.fori_loop(1, 8, send_b1, 0)
-    packed = dot(pack_a, xbf).astype(BF16)
-    apack[...] = packed.reshape(16, 16, 512)
-    arecv[me] = apack[me]
-
-    for dy, dz in PLANE:
-        step = dy * 4 + dz
-        peer, device = plane(step)
-        remote(apack.at[peer], arecv.at[me], a1s, a1r, device).start()
-
-    whole(xb1, 7, b1s, b1r).wait_recv()
-    xb_all = xb1[...].reshape(128, 512)
-    for i in range(2):
-        pick = jnp.where(((ll & 15) >> 2) == core * 2 + i, pack_b, 0.0).astype(BF16)
-        bpack[:, :, i * 512 : (i + 1) * 512] = (
-            dot(pick, xb_all).astype(BF16).reshape(16, 16, 512)
-        )
-    xbh[core, me] = bpack[me]
-
-    for dy, dz in PLANE:
-        step = dy * 4 + dz
-        peer, device = plane(step)
-        remote(bpack.at[peer], xbh.at[core, me], b2s, b2r, device).start()
-
-    whole(arecv, 15, a1s, a1r).wait_recv()
+    for h, (xs, apack, arecv) in enumerate(((xsa0, apack0, arecv0), (xsa1, apack1, arecv1))):
+        packed = dot(pack_a, xs[...].astype(BF16)).astype(BF16)
+        apack[...] = packed.reshape(16, 16, packed.shape[1])
+        arecv[me] = apack[me]
+        for dy, dz in PLANE:
+            peer, device = plane(dy * 4 + dz)
+            remote(apack.at[peer], arecv.at[me], a1s.at[h], a1r.at[h], device).start()
+
     rr = iota((256, 256), 0)
     ll = iota((256, 256), 1)
     unpack_a = onehot(ll == (rr & 31) * 8 + (rr >> 5))
-    got = dot(unpack_a, arecv[...].reshape(256, 512)).astype(BF16)
-    for p in range(8):
-        xa[p // 2, core, x, :, (p % 2) * 512 : (p % 2) * 512 + 512] = got[p * 32 : p * 32 + 32, :]
+
+    def arrive_a(h):
+        arecv = (arecv0, arecv1)[h]
+        first, chunks = IN_PARTS[h]
+        width = chunks * CHUNK // 8
+        whole(arecv, 15, a1s.at[h], a1r.at[h]).wait_recv()
+        got = dot(unpack_a, arecv[...].reshape(256, width)).astype(BF16)
+        for p in range(8):
+            n, start = divmod(p * width, CHUNK)
+            xa[first + n, core, x, :, start : start + width] = got[p * 32 : p * 32 + 32, :]
 
     def near_in(n):
         mine_ref = xa.at[n, core, x]
@@ -371,85 +408,126 @@
         b = remote(high, high, fs, fr.at[1, n], left_dev)
         return a, b
 
-    def core_send(n):
-        half = xa.at[n, core]
-        return remote(half, half, acs, acr.at[n], other_dev)
+    def core_send(n, place):
+        block = xa.at[n, core, place]
+        remote(block, block, acs, acr.at[n], other_dev).start()
 
     def core_arrival(n):
         half = xa.at[n, 1 - core]
         return remote(half, half, acs, acr.at[n], other_dev)
 
-    for n in range(A_CHUNKS):
+    def near_send(n):
         for copy in near_in(n):
             copy.start()
-
-    accg[...] = jnp.zeros((256, HIDDEN), F32)
-    accu[...] = jnp.zeros((256, HIDDEN), F32)
+        core_send(n, x)
+
+    def wait_rows():
+        whole(xb1, 7, b1s, b1r).wait_recv()
+
+    def send_b2(i):
+        lane = iota((256, 128), 1)
+        pick = jnp.where(((lane & 15) >> 2) == core * 2 + i, pack_b, 0.0).astype(BF16)
+        bpack[i] = dot(pick, xb1[...].reshape(128, PIECE)).astype(BF16).reshape(16, 16, PIECE)
+        xbh[i, core, me] = bpack[i, me]
+        for dy, dz in PLANE:
+            peer, device = plane(dy * 4 + dz)
+            remote(
+                bpack.at[i, peer], xbh.at[i, core, me], b2s.at[i], b2r.at[i], device
+            ).start()
+
+    arrive_a(0)
+    near_send(0)
+    wait_rows()
+    send_b2(0)
+    arrive_a(1)
+    near_send(1)
+    accg[...] = jnp.zeros((HIDDEN, 256), F32)
+    accu[...] = jnp.zeros((HIDDEN, 256), F32)
     pltpu.make_async_copy(wg_hbm.at[0], wg, local_sem.at[2]).wait()
     pltpu.make_async_copy(wu_hbm.at[0], wu, local_sem.at[3]).wait()
 
     def project(value, offset):
-        cols = pl.ds(offset, CHUNK)
-        accg[...] += dot_nt(value, wg[:, cols])
-        accu[...] += dot_nt(value, wu[:, cols])
+        cols = pl.ds(offset, value.shape[1])
+        accg[...] += dot_nt(wg[:, cols], value)
+        accu[...] += dot_nt(wu[:, cols], value)
 
     def project_a(n):
         core_arrival(n).wait_recv()
         project(xa[n].reshape(256, CHUNK), n * CHUNK)
 
     def relay(n):
-        for copy in near_arrivals(n):
-            copy.wait_recv()
-        for copy in far_sends(n):
-            copy.start()
+        for arrival, send, place in zip(near_arrivals(n), far_sends(n), (left, right)):
+            arrival.wait_recv()
+            send.start()
+            core_send(n, place)
 
     def forward(n):
         for copy in far_arrivals(n):
             copy.wait_recv()
-        core_send(n).start()
-
-    for n in range(A_CHUNKS):
-        relay(n)
-    forward(0)
-
-    whole(xbh.at[core], 15, b2s, b2r).wait_recv()
-    bcore = remote(xbh.at[core], xbh.at[core], bcs, bcr, other_dev)
-    bcore.start()
-    forward(1)
+        core_send(n, opposite)
+
+    def b2_core(i):
+        return remote(xbh.at[i, core], xbh.at[i, core], bcs, bcr.at[i], other_dev)
+
+    def forward_b(i):
+        whole(xbh.at[i, core], 15, b2s.at[i], b2r.at[i]).wait_recv()
+        b2_core(i).start()
+
     tau = rr >> 5
     unpack_b = onehot(
         ll == ((rr & 31) >> 1) * 16 + ((tau & 3) * 2 + (tau >> 2)) * 2 + (rr & 1)
     )
 
-    def project_b(half):
-        offset = pl.multiple_of(A_COLS + half * CHUNK, CHUNK)
-        project(dot(unpack_b, xbh[half].reshape(256, CHUNK)).astype(BF16), offset)
-
+    def project_b(half, i):
+        offset = pl.multiple_of(IN_A + half * 2 * PIECE + i * PIECE, PIECE)
+        project(dot(unpack_b, xbh[i, half].reshape(256, PIECE)).astype(BF16), offset)
+
+    def project_own(i):
+        project_b(core, i)
+
+    def project_other(i):
+        remote(
+            xbh.at[i, 1 - core], xbh.at[i, 1 - core], bcs, bcr.at[i], other_dev
+        ).wait_recv()
+        project_b(1 - core, i)
+
+    relay(0)
+    near_send(2)
+    send_b2(1)
+    relay(1)
+    forward(0)
+    forward_b(0)
+    relay(2)
     project_a(0)
-    project_b(core)
+    project_own(0)
+    forward(1)
+    project_other(0)
+    project_a(1)
     forward(2)
-    project_a(1)
-    forward(3)
-    remote(xbh.at[1 - core], xbh.at[1 - core], bcs, bcr, other_dev).wait_recv()
-    project_b(1 - core)
+    forward_b(1)
+    project_own(1)
     project_a(2)
-    project_a(3)
+    project_other(1)
     g = accg[...]
     hidden = (g * jax.nn.sigmoid(g) * accu[...]).astype(BF16)
-    hid[...] = hidden
+    hid[...] = dot_nt(onehot(rr == ll), hidden).astype(BF16)
     t_of = (rr & 15) >> 1
     to_b = onehot(ll == ((t_of & 1) * 4 + (t_of >> 1)) * 32 + (rr >> 4) * 2 + (rr & 1))
-    hidb[...] = dot(to_b, hidden).astype(BF16)
     pltpu.make_async_copy(wd_hbm.at[0], wd, local_sem.at[4]).wait()
 
     def drain():
         whole(xb1, 7, b1s, b1r).wait_send()
-        whole(arecv, 15, a1s, a1r).wait_send()
-        whole(xbh.at[core], 15, b2s, b2r).wait_send()
-        bcore.wait_send()
-        remote(xa.at[0], xa.at[0], ns, nr.at[0, 0], other_dev).wait_send()
-        remote(xa.at[0, 0], xa.at[0, 0], fs, fr.at[0, 0], other_dev).wait_send()
-        remote(xa.at[0:2], xa.at[0:2], acs, acr.at[0], other_dev).wait_send()
+        whole(arecv0, 15, a1s.at[0], a1r.at[0]).wait_send()
+        whole(arecv1, 15, a1s.at[1], a1r.at[1]).wait_send()
+        for i in range(2):
+            whole(xbh.at[i, core], 15, b2s.at[i], b2r.at[i]).wait_send()
+        remote(xbh.at[0:2, 0], xbh.at[0:2, 0], bcs, bcr.at[0], other_dev).wait_send()
+        sent = xa.at[0:IN_CHUNKS, 0, 0:2]
+        remote(sent, sent, ns, nr.at[0, 0], other_dev).wait_send()
+        sent = xa.at[0:IN_CHUNKS, 0, 0]
+        remote(sent, sent, fs, fr.at[0, 0], other_dev).wait_send()
+        sent = xa.at[0:IN_CHUNKS, 0]
+        remote(sent, sent, acs, acr.at[0], other_dev).wait_send()
         remote(cr, cr, rcs, rcr.at[0], other_dev).wait_send()
         b_core().wait_send()
         whole(bback, 15, rbs, rbr).wait_send()
@@ -501,45 +579,65 @@
         rows = pl.ds(pl.multiple_of(x * 32, 32), 32)
         y = pm[n, rows, :] + near[0, n].astype(F32) + near[1, n].astype(F32)
         y = y.astype(BF16)
-        for p in range(2):
-            y2[(n * 2 + p) * 32 : (n * 2 + p) * 32 + 32, :] = y[:, p * 512 : p * 512 + 512]
+        for q in range(4):
+            row = ((n % 2) * 4 + q) * 32
+            y2[n // 2, row : row + 32, :] = y[:, q * 256 : q * 256 + 256]
 
     def b_core():
         return remote(pbs, cbr, rbcs, rbcr, other_dev)
 
-    b0 = dot(hidb[...], wd[:, A_COLS : A_COLS + CHUNK])
-    b1 = dot(hidb[...], wd[:, A_COLS + CHUNK : A_COLS + 2 * CHUNK])
-    pbs[...] = jnp.where(core == 0, b1, b0).astype(BF16)
-    pbm[...] = jnp.where(core == 0, b0, b1)
-    b_core().start()
+    def down_b(half):
+        cols = pl.ds(pl.multiple_of(A_COLS + half * CHUNK, CHUNK), CHUNK)
+        return dot(hidb[...], wd[:, cols])
+
+    def b_other():
+        hidb[...] = dot_nt(to_b, hidden).astype(BF16)
+        pbs[...] = down_b(1 - core).astype(BF16)
+        b_core().start()
+
+    def b_mine():
+        pbm[...] = down_b(core)
+
+    def b_home():
+        b_core().wait_recv()
+        bsend[...] = (pbm[...] + cbr[...].astype(F32)).astype(BF16).reshape(16, 16, CHUNK)
+        bback[me] = bsend[me]
+        for dy, dz in PLANE:
+            peer, device = plane(dy * 4 + dz)
+            remote(bsend.at[peer], bback.at[me], rbs, rbr, device).start()
+
+    rr = iota((256, 256), 0)
+    ll = iota((256, 256), 1)
+    repack_a = onehot(ll == (rr & 7) * 32 + (rr >> 3))
+
+    def a_home(h):
+        asend[h] = dot(repack_a, y2[h]).astype(BF16).reshape(16, 16, 256)
+        aback[h, me] = asend[h, me]
+        for dy, dz in PLANE:
+            peer, device = plane(dy * 4 + dz)
+            remote(asend.at[h, peer], aback.at[h, me], ras.at[h], rar.at[h], device).start()
+
     down_a(0)
     down_a(1)
     chip_sum(0)
-    b_core().wait_recv()
-    bsend[...] = (pbm[...] + cbr[...].astype(F32)).astype(BF16).reshape(16, 16, CHUNK)
-    bback[me] = bsend[me]
-    for dy, dz in PLANE:
-        step = dy * 4 + dz
-        peer, device = plane(step)
-        remote(bsend.at[peer], bback.at[me], rbs, rbr, device).start()
+    b_other()
     down_a(2)
     chip_sum(1)
     down_a(3)
     chip_sum(2)
+    ret_relay(0)
+    b_mine()
     chip_sum(3)
-    for n in range(A_CHUNKS):
-        ret_relay(n)
-    for n in range(A_CHUNKS):
-        ret_sum(n)
-    rr = iota((256, 256), 0)
-    ll = iota((256, 256), 1)
-    repack_a = onehot(ll == (rr & 7) * 32 + (rr >> 3))
-    asend[...] = dot(repack_a, y2[...]).astype(BF16).reshape(16, 16, 512)
-    aback[me] = asend[me]
-    for dy, dz in PLANE:
-        step = dy * 4 + dz
-        peer, device = plane(step)
-        remote(asend.at[peer], aback.at[me], ras, rar, device).start()
+    b_home()
+    ret_relay(1)
+    ret_relay(2)
+    ret_relay(3)
+    ret_sum(0)
+    ret_sum(1)
+    a_home(0)
+    ret_sum(2)
+    ret_sum(3)
+    a_home(1)
 
     rr = iota((128, 256), 0)
     ll = iota((128, 256), 1)
@@ -580,20 +678,21 @@
     rr = iota((64, 256), 0)
     ll = iota((64, 256), 1)
     keep = (rr >> 3) == (ll & 7)
-    home_hi = dot_nt(dot_nt(mine[0:64], whi).astype(BF16), spread_a)
-    home_lo = dot_nt(dot_nt(mine[0:64], wlo).astype(BF16), spread_a)
+    home_hi = dot_nt(dot_nt(mine, whi).astype(BF16), spread_a)
+    home_lo = dot_nt(dot_nt(mine, wlo).astype(BF16), spread_a)
     home_hi = jnp.where(keep, home_hi, 0.0).astype(BF16)
     home_lo = jnp.where(keep, home_lo, 0.0).astype(BF16)
 
     drain()
-    whole(aback, 15, ras, rar).wait_recv()
-    back = aback[...].reshape(256, 512)
-    home_a = dot(home_hi, back) + dot(home_lo, back)
-    for p in range(8):
-        cols = slice(p * 512, p * 512 + 512)
-        out[:, cols] = (stream[0:4, cols] + home_a[p * 8 : p * 8 + 4, :]).astype(BF16)
-
-    whole(aback, 15, ras, rar).wait_send()
+    for h in range(2):
+        whole(aback.at[h], 15, ras.at[h], rar.at[h]).wait_recv()
+        back = aback[h].reshape(256, 256)
+        home_a = dot(home_hi, back) + dot(home_lo, back)
+        for p in range(8):
+            cols = slice(h * 2048 + p * 256, h * 2048 + p * 256 + 256)
+            out[:, cols] = (stream[0:4, cols] + home_a[p * 8 : p * 8 + 4, :]).astype(BF16)
+    for h in range(2):
+        whole(aback.at[h], 15, ras.at[h], rar.at[h]).wait_send()
 
 
 def layer(
@@ -616,6 +715,14 @@
     dma = pltpu.SemaphoreType.DMA
     n = A_CHUNKS
     scratch = [
+        pltpu.SMEM((ROWS,), jnp.int32),
+        pltpu.VMEM((ROWS, D), BF16),
+        pltpu.VMEM((ROWS, D), BF16),
+        pltpu.VMEM((ROWS, 1024), BF16),
+        pltpu.VMEM((ROWS, 1024), BF16),
+        pltpu.VMEM((1, D), F32),
+        pltpu.VMEM((4, 32), jnp.int32),
+        pltpu.VMEM((4, 32), jnp.int32),
         pltpu.VMEM((ROWS, LENGTH, 1024), BF16),
         pltpu.VMEM((ROWS, LENGTH, 1024), BF16),
         pltpu.VMEM((HIDDEN, D), BF16),
@@ -627,16 +734,20 @@
         pltpu.VMEM((GROUP * ROWS, 1024), F32),
         pltpu.VMEM((HEADS * ROWS, 128), F32),
         pltpu.VMEM((8, D), F32),
-        pltpu.VMEM((96, 512), F32),
-        pltpu.VMEM((16, 16, 512), BF16),
-        pltpu.VMEM((16, 16, 512), BF16),
-        pltpu.VMEM((16, 512), BF16),
-        pltpu.VMEM((8, 16, 512), BF16),
-        pltpu.VMEM((16, 16, CHUNK), BF16),
-        pltpu.VMEM((2, 16, 16, CHUNK), BF16),
-        pltpu.VMEM((n, 2, 4, 32, CHUNK), BF16),
-        pltpu.VMEM((256, HIDDEN), F32),
-        pltpu.VMEM((256, HIDDEN), F32),
+        pltpu.VMEM((64, 128), F32),
+        pltpu.VMEM((64, 256), F32),
+        pltpu.VMEM((32, PIECE), F32),
+        pltpu.VMEM((16, 16, 128), BF16),
+        pltpu.VMEM((16, 16, 256), BF16),
+        pltpu.VMEM((16, 16, 128), BF16),
+        pltpu.VMEM((16, 16, 256), BF16),
+        pltpu.VMEM((16, PIECE), BF16),
+        pltpu.VMEM((8, 16, PIECE), BF16),
+        pltpu.VMEM((2, 16, 16, PIECE), BF16),
+        pltpu.VMEM((2, 2, 16, 16, PIECE), BF16),
+        pltpu.VMEM((IN_CHUNKS, 2, 4, 32, CHUNK), BF16),
+        pltpu.VMEM((HIDDEN, 256), F32),
+        pltpu.VMEM((HIDDEN, 256), F32),
         pltpu.VMEM((256, HIDDEN), BF16),
         pltpu.VMEM((256, HIDDEN), BF16),
         pltpu.VMEM((n, 2, 128, CHUNK), BF16),
@@ -645,9 +756,9 @@
         pltpu.VMEM((n, 4, 32, CHUNK), BF16),
         pltpu.VMEM((2, n, 16, CHUNK), BF16),
         pltpu.VMEM((2, n, 32, CHUNK), BF16),
-        pltpu.VMEM((256, 512), BF16),
-        pltpu.VMEM((16, 16, 512), BF16),
-        pltpu.VMEM((16, 16, 512), BF16),
+        pltpu.VMEM((2, 256, 256), BF16),
+        pltpu.VMEM((2, 16, 16, 256), BF16),
+        pltpu.VMEM((2, 16, 16, 256), BF16),
         pltpu.VMEM((256, CHUNK), BF16),
         pltpu.VMEM((256, CHUNK), F32),
         pltpu.VMEM((256, CHUNK), BF16),
@@ -655,15 +766,15 @@
         pltpu.VMEM((16, 16, CHUNK), BF16),
         pltpu.VMEM((8, 16, 256), BF16),
         pltpu.VMEM((8, 16, 256), BF16),
-        dma((5,)),
-        dma,
-        dma,
-        dma,
-        dma,
-        dma,
-        dma,
-        dma,
-        dma,
+        dma((13,)),
+        dma((2,)),
+        dma((2,)),
+        dma,
+        dma,
+        dma((2,)),
+        dma((2,)),
+        dma,
+        dma((2,)),
         dma,
         dma((2, n)),
         dma,
@@ -676,8 +787,8 @@
         dma((2, n)),
         dma,
         dma((2, n)),
-        dma,
-        dma,
+        dma((2,)),
+        dma((2,)),
         dma,
         dma,
         dma,
@@ -688,7 +799,7 @@
     return pl.pallas_call(
         kernel,
         out_shape=jax.ShapeDtypeStruct((ROWS, D), BF16),
-        in_specs=[pl.BlockSpec(memory_space=pltpu.SMEM)] + [vmem] * 7 + [anywhere] * 5,
+        in_specs=[anywhere] * 13,
         out_specs=vmem,
         scratch_shapes=scratch,
         compiler_params=pltpu.CompilerParams(

time: 56.7 us -> 54.1 us (0.954)
  the two profiles are of different devices: /device:TPU:0 before, /device:TPU:1 now
where the time goes in v3:
time: 54.1 us; the launch traced here: 54 us
  Pallas kernels  52.5 us (97%)
  local copies, waits for them, and re-layouts  1.44 us (3%)
    pallas_call x1, Pallas kernels, layer(): pl.pallas_call(kernel, out_shape=jax.ShapeDtypeStruct((ROWS, D), BF16), i...  52.5 us
    unnamed x1, local copies, waits for them, and re-layouts  1.44 us

profile of v3, /device:TPU:1, one launch (start us, length us, event | category | flops | bytes accessed | tf_op | source)
XLA Modules:
  0.0 54.0 jit_solution(4842935598760074657)
XLA Ops:
  0.0 52.5 %shard_map.127 = bf16[4,6144]{1,0:T(4,128)(2,1)} custom-call(s32[4]{0:T(128)} %clen_hbm.1, bf16[4,6144]{1,0:T(4,128)(2,1)} %resid_hbm.1, bf16[4,6144]{1,0:T(4,128)(2,1)} %query_hbm.1, bf16[4,1024]{1,0:T(4,128)(2,1)} %new_key_hbm.1, bf16[4,1024]{1,0:T(4,128)(2,1)} %new_value_hbm.1, f32[1,6144]{1,0:T(1,128)} %bitcast.3, s32[4,32]{1,0:T(4,128)} %bitcast.4, ...), custom_call_target="tpu_custom_call" | custom-call | flops 6341787648 | bytes 28311552 | tf_op jit(solution)/shard_map/pallas_call | solution.py:799
  52.5 1.4 %copy.15 = bf16[4,6144]{1,0:T(4,128)(2,1)} copy(bf16[4,6144]{1,0:T(4,128)(2,1)} %shard_map.127) | data formatting | bytes 98304

commit v4 on v3

--- a/solution.py
+++ b/solution.py
@@ -20,6 +20,7 @@
 IN_A = IN_CHUNKS * CHUNK
 IN_PARTS = ((0, 1), (1, 2))
 PIECE = (D - IN_A) // 4
+B_PARTS = ((0, 0, 256), (0, 256, 512), (1, 0, 768))
 A_CHUNKS = 4
 A_COLS = A_CHUNKS * CHUNK
 F32 = jnp.float32
@@ -100,8 +101,12 @@
     arecv1,
     bmsg,
     xb1,
-    bpack,
-    xbh,
+    bpack0,
+    bpack1,
+    bpack2,
+    xbh0,
+    xbh1,
+    xbh2,
     xa,
     accg,
     accu,
@@ -182,6 +187,8 @@
         part = buffer.at[pl.ds(0, count)]
         return remote(part, part, send_sem, recv_sem, other_dev)
 
+    bpacks = (bpack0, bpack1, bpack2)
+    xbhs = (xbh0, xbh1, xbh2)
     barrier = pltpu.get_barrier_semaphore()
 
     def greet_plane(step, carry):
@@ -424,16 +431,17 @@
     def wait_rows():
         whole(xb1, 7, b1s, b1r).wait_recv()
 
-    def send_b2(i):
+    def send_b2(k):
+        i, start, width = B_PARTS[k]
+        bpack, xbh = bpacks[k], xbhs[k]
         lane = iota((256, 128), 1)
         pick = jnp.where(((lane & 15) >> 2) == core * 2 + i, pack_b, 0.0).astype(BF16)
-        bpack[i] = dot(pick, xb1[...].reshape(128, PIECE)).astype(BF16).reshape(16, 16, PIECE)
-        xbh[i, core, me] = bpack[i, me]
+        piece = xb1[:, :, start : start + width].reshape(128, width)
+        bpack[...] = dot(pick, piece).astype(BF16).reshape(16, 16, width)
+        xbh[core, me] = bpack[me]
         for dy, dz in PLANE:
             peer, device = plane(dy * 4 + dz)
-            remote(
-                bpack.at[i, peer], xbh.at[i, core, me], b2s.at[i], b2r.at[i], device
-            ).start()
+            remote(bpack.at[peer], xbh.at[core, me], b2s.at[k], b2r.at[k], device).start()
 
     arrive_a(0)
     near_send(0)
@@ -441,6 +449,7 @@
     send_b2(0)
     arrive_a(1)
     near_send(1)
+    send_b2(1)
     accg[...] = jnp.zeros((HIDDEN, 256), F32)
     accu[...] = jnp.zeros((HIDDEN, 256), F32)
     pltpu.make_async_copy(wg_hbm.at[0], wg, local_sem.at[2]).wait()
@@ -466,48 +475,51 @@
             copy.wait_recv()
         core_send(n, opposite)
 
-    def b2_core(i):
-        return remote(xbh.at[i, core], xbh.at[i, core], bcs, bcr.at[i], other_dev)
-
-    def forward_b(i):
-        whole(xbh.at[i, core], 15, b2s.at[i], b2r.at[i]).wait_recv()
-        b2_core(i).start()
+    def b2_core(k, half):
+        block = xbhs[k].at[half]
+        return remote(block, block, bcs.at[k], bcr.at[k], other_dev)
+
+    def forward_b(k):
+        whole(xbhs[k].at[core], 15, b2s.at[k], b2r.at[k]).wait_recv()
+        b2_core(k, core).start()
 
     tau = rr >> 5
     unpack_b = onehot(
         ll == ((rr & 31) >> 1) * 16 + ((tau & 3) * 2 + (tau >> 2)) * 2 + (rr & 1)
     )
 
-    def project_b(half, i):
-        offset = pl.multiple_of(IN_A + half * 2 * PIECE + i * PIECE, PIECE)
-        project(dot(unpack_b, xbh[i, half].reshape(256, PIECE)).astype(BF16), offset)
-
-    def project_own(i):
-        project_b(core, i)
-
-    def project_other(i):
-        remote(
-            xbh.at[i, 1 - core], xbh.at[i, 1 - core], bcs, bcr.at[i], other_dev
-        ).wait_recv()
-        project_b(1 - core, i)
+    def project_b(half, k):
+        i, start, width = B_PARTS[k]
+        offset = pl.multiple_of(IN_A + half * 2 * PIECE + i * PIECE + start, 256)
+        project(dot(unpack_b, xbhs[k][half].reshape(256, width)).astype(BF16), offset)
+
+    def project_own(k):
+        project_b(core, k)
+
+    def project_other(k):
+        b2_core(k, 1 - core).wait_recv()
+        project_b(1 - core, k)
 
     relay(0)
     near_send(2)
-    send_b2(1)
+    send_b2(2)
     relay(1)
+    forward_b(0)
+    project_own(0)
     forward(0)
-    forward_b(0)
     relay(2)
+    forward_b(1)
+    project_other(0)
+    project_own(1)
+    forward(1)
     project_a(0)
-    project_own(0)
-    forward(1)
-    project_other(0)
+    project_other(1)
+    forward(2)
     project_a(1)
-    forward(2)
-    forward_b(1)
-    project_own(1)
+    forward_b(2)
+    project_own(2)
     project_a(2)
-    project_other(1)
+    project_other(2)
     g = accg[...]
     hidden = (g * jax.nn.sigmoid(g) * accu[...]).astype(BF16)
     hid[...] = dot_nt(onehot(rr == ll), hidden).astype(BF16)
@@ -519,9 +531,9 @@
         whole(xb1, 7, b1s, b1r).wait_send()
         whole(arecv0, 15, a1s.at[0], a1r.at[0]).wait_send()
         whole(arecv1, 15, a1s.at[1], a1r.at[1]).wait_send()
-        for i in range(2):
-            whole(xbh.at[i, core], 15, b2s.at[i], b2r.at[i]).wait_send()
-        remote(xbh.at[0:2, 0], xbh.at[0:2, 0], bcs, bcr.at[0], other_dev).wait_send()
+        for k in range(3):
+            whole(xbhs[k].at[core], 15, b2s.at[k], b2r.at[k]).wait_send()
+            b2_core(k, core).wait_send()
         sent = xa.at[0:IN_CHUNKS, 0, 0:2]
         remote(sent, sent, ns, nr.at[0, 0], other_dev).wait_send()
         sent = xa.at[0:IN_CHUNKS, 0, 0]
@@ -617,18 +629,18 @@
             peer, device = plane(dy * 4 + dz)
             remote(asend.at[h, peer], aback.at[h, me], ras.at[h], rar.at[h], device).start()
 
+    b_other()
     down_a(0)
     down_a(1)
+    b_mine()
     chip_sum(0)
-    b_other()
     down_a(2)
     chip_sum(1)
+    b_home()
     down_a(3)
     chip_sum(2)
+    chip_sum(3)
     ret_relay(0)
-    b_mine()
-    chip_sum(3)
-    b_home()
     ret_relay(1)
     ret_relay(2)
     ret_relay(3)
@@ -636,8 +648,6 @@
     ret_sum(1)
     a_home(0)
     ret_sum(2)
-    ret_sum(3)
-    a_home(1)
 
     rr = iota((128, 256), 0)
     ll = iota((128, 256), 1)
@@ -660,6 +670,8 @@
         return carry
 
     lax.fori_loop(1, 8, send_b4, 0)
+    ret_sum(3)
+    a_home(1)
     whole(frecv, 7, rfis, rfir).wait_recv()
     rr = iota((64, 128), 0)
     ll = iota((64, 128), 1)
@@ -743,8 +755,8 @@
         pltpu.VMEM((16, 16, 256), BF16),
         pltpu.VMEM((16, PIECE), BF16),
         pltpu.VMEM((8, 16, PIECE), BF16),
-        pltpu.VMEM((2, 16, 16, PIECE), BF16),
-        pltpu.VMEM((2, 2, 16, 16, PIECE), BF16),
+        *[pltpu.VMEM((16, 16, width), BF16) for _, _, width in B_PARTS],
+        *[pltpu.VMEM((2, 16, 16, width), BF16) for _, _, width in B_PARTS],
         pltpu.VMEM((IN_CHUNKS, 2, 4, 32, CHUNK), BF16),
         pltpu.VMEM((HIDDEN, 256), F32),
         pltpu.VMEM((HIDDEN, 256), F32),
@@ -771,10 +783,10 @@
         dma((2,)),
         dma,
         dma,
-        dma((2,)),
-        dma((2,)),
-        dma,
-        dma((2,)),
+        dma((3,)),
+        dma((3,)),
+        dma((3,)),
+        dma((3,)),
         dma,
         dma((2, n)),
         dma,

time: 54.1 us -> 52.2 us (0.965)
  the two profiles are of different devices: /device:TPU:1 before, /device:TPU:0 now
where the time goes in v4:
time: 52.2 us; the launch traced here: 52 us
  Pallas kernels  50.6 us (97%)
  local copies, waits for them, and re-layouts  1.44 us (3%)
    pallas_call x1, Pallas kernels, layer(): pl.pallas_call(kernel, out_shape=jax.ShapeDtypeStruct((ROWS, D), BF16), i...  50.6 us
    unnamed x1, local copies, waits for them, and re-layouts  1.44 us

profile of v4, /device:TPU:0, one launch (start us, length us, event | category | flops | bytes accessed | tf_op | source)
XLA Modules:
  0.0 52.0 jit_solution(7452135196523161632)
XLA Ops:
  0.0 50.6 %shard_map.127 = bf16[4,6144]{1,0:T(4,128)(2,1)} custom-call(s32[4]{0:T(128)} %clen_hbm.1, bf16[4,6144]{1,0:T(4,128)(2,1)} %resid_hbm.1, bf16[4,6144]{1,0:T(4,128)(2,1)} %query_hbm.1, bf16[4,1024]{1,0:T(4,128)(2,1)} %new_key_hbm.1, bf16[4,1024]{1,0:T(4,128)(2,1)} %new_value_hbm.1, f32[1,6144]{1,0:T(1,128)} %bitcast.3, s32[4,32]{1,0:T(4,128)} %bitcast.4, ...), custom_call_target="tpu_custom_call" | custom-call | flops 6341787648 | bytes 28311552 | tf_op jit(solution)/shard_map/pallas_call | solution.py:811
  50.6 1.4 %copy.15 = bf16[4,6144]{1,0:T(4,128)(2,1)} copy(bf16[4,6144]{1,0:T(4,128)(2,1)} %shard_map.127) | data formatting | bytes 98304

commit v5 on v4

--- a/solution.py
+++ b/solution.py
@@ -23,6 +23,7 @@
 B_PARTS = ((0, 0, 256), (0, 256, 512), (1, 0, 768))
 A_CHUNKS = 4
 A_COLS = A_CHUNKS * CHUNK
+OUT_PARTS = ((0, 2), (2, 1), (3, 1))
 F32 = jnp.float32
 BF16 = jnp.bfloat16
 MESH = pl.DeviceIdType.MESH
@@ -118,9 +119,15 @@
     cs,
     far,
     near,
-    y2,
-    asend,
-    aback,
+    y20,
+    y21,
+    y22,
+    asend0,
+    asend1,
+    asend2,
+    aback0,
+    aback1,
+    aback2,
     pbs,
     pbm,
     cbr,
@@ -128,6 +135,9 @@
     bback,
     fsend,
     frecv,
+    mix_a,
+    mix_b,
+    gather,
     local_sem,
     a1s,
     a1r,
@@ -188,6 +198,9 @@
         return remote(part, part, send_sem, recv_sem, other_dev)
 
     bpacks = (bpack0, bpack1, bpack2)
+    y2s = (y20, y21, y22)
+    asends = (asend0, asend1, asend2)
+    abacks = (aback0, aback1, aback2)
     xbhs = (xbh0, xbh1, xbh2)
     barrier = pltpu.get_barrier_semaphore()
 
@@ -506,16 +519,31 @@
     relay(1)
     forward_b(0)
     project_own(0)
-    forward(0)
-    relay(2)
-    forward_b(1)
+
+    @pl.when(core == 1)
+    def early():
+        forward(0)
+        relay(2)
+        forward_b(1)
+
     project_other(0)
+
+    @pl.when(core == 0)
+    def late():
+        forward(0)
+
+    project_a(0)
+
+    @pl.when(core == 0)
+    def later():
+        relay(2)
+        forward_b(1)
+
     project_own(1)
     forward(1)
-    project_a(0)
     project_other(1)
+    project_a(1)
     forward(2)
-    project_a(1)
     forward_b(2)
     project_own(2)
     project_a(2)
@@ -543,8 +571,8 @@
         remote(cr, cr, rcs, rcr.at[0], other_dev).wait_send()
         b_core().wait_send()
         whole(bback, 15, rbs, rbr).wait_send()
-        remote(far, far, rfs, rfr.at[0, 0], other_dev).wait_send()
-        remote(near, near, rns, rnr.at[0, 0], other_dev).wait_send()
+        remote(far, far, rfs, rfr.at[0], other_dev).wait_send()
+        remote(near, near, rns, rnr.at[0], other_dev).wait_send()
         whole(frecv, 7, rfis, rfir).wait_send()
 
     def down_a(n):
@@ -563,21 +591,21 @@
 
     def ret_far(n):
         a = remote(
-            cs.at[n, opposite, pl.ds(0, 16), :], far.at[0, n], rfs, rfr.at[0, n], right_dev
+            cs.at[n, opposite, pl.ds(0, 16), :], far.at[0, n], rfs, rfr.at[n], right_dev
         )
         b = remote(
-            cs.at[n, opposite, pl.ds(16, 16), :], far.at[1, n], rfs, rfr.at[1, n], left_dev
+            cs.at[n, opposite, pl.ds(16, 16), :], far.at[1, n], rfs, rfr.at[n], left_dev
         )
         return a, b
 
     def ret_near(n):
-        a = remote(cs.at[n, right], near.at[0, n], rns, rnr.at[0, n], right_dev)
-        b = remote(cs.at[n, left], near.at[1, n], rns, rnr.at[1, n], left_dev)
+        a = remote(cs.at[n, right], near.at[0, n], rns, rnr.at[n], right_dev)
+        b = remote(cs.at[n, left], near.at[1, n], rns, rnr.at[n], left_dev)
         return a, b
 
     def ret_relay(n):
-        for copy in ret_far(n):
-            copy.wait_recv()
+        both = near.at[0, n]
+        remote(both, both, rfs, rfr.at[n], right_dev).wait_recv()
         to_right = pl.ds(pl.multiple_of(right * 32, 32), 16)
         to_left = pl.ds(pl.multiple_of(left * 32 + 16, 16), 16)
         cs[n, right, 0:16, :] = (pm[n, to_right, :] + far[0, n].astype(F32)).astype(BF16)
@@ -586,14 +614,17 @@
             copy.start()
 
     def ret_sum(n):
-        for copy in ret_near(n):
-            copy.wait_recv()
+        both = pa.at[n, 0, 0:64]
+        remote(both, both, rns, rnr.at[n], right_dev).wait_recv()
         rows = pl.ds(pl.multiple_of(x * 32, 32), 32)
         y = pm[n, rows, :] + near[0, n].astype(F32) + near[1, n].astype(F32)
         y = y.astype(BF16)
-        for q in range(4):
-            row = ((n % 2) * 4 + q) * 32
-            y2[n // 2, row : row + 32, :] = y[:, q * 256 : q * 256 + 256]
+        for (first, chunks), y2 in zip(OUT_PARTS, y2s):
+            if first <= n < first + chunks:
+                width = chunks * CHUNK // 8
+                for q in range(CHUNK // width):
+                    row = ((n - first) * (CHUNK // width) + q) * 32
+                    y2[row : row + 32, :] = y[:, q * width : (q + 1) * width]
 
     def b_core():
         return remote(pbs, cbr, rbcs, rbcr, other_dev)
@@ -623,44 +654,65 @@
     repack_a = onehot(ll == (rr & 7) * 32 + (rr >> 3))
 
     def a_home(h):
-        asend[h] = dot(repack_a, y2[h]).astype(BF16).reshape(16, 16, 256)
-        aback[h, me] = asend[h, me]
+        asend, aback = asends[h], abacks[h]
+        value = dot(repack_a, y2s[h][...]).astype(BF16)
+        asend[...] = value.reshape(16, 16, value.shape[1])
+        aback[me] = asend[me]
         for dy, dz in PLANE:
             peer, device = plane(dy * 4 + dz)
-            remote(asend.at[h, peer], aback.at[h, me], ras.at[h], rar.at[h], device).start()
-
+            remote(asend.at[peer], aback.at[me], ras.at[h], rar.at[h], device).start()
+
+    def home_tables():
+        rr = iota((128, 256), 0)
+        ll = iota((128, 256), 1)
+        wide_hi = dot_nt(dot_nt(wide, whi).astype(BF16), spread_b)
+        wide_lo = dot_nt(dot_nt(wide, wlo).astype(BF16), spread_b)
+        for q in range(4):
+            keep = ((rr >> 4) == ((ll & 15) >> 1)) & (((rr & 15) >> 2) == q)
+            mix_b[2 * q] = jnp.where(keep, wide_hi, 0.0).astype(BF16)
+            mix_b[2 * q + 1] = jnp.where(keep, wide_lo, 0.0).astype(BF16)
+        rr = iota((64, 256), 0)
+        ll = iota((64, 256), 1)
+        keep = (rr >> 3) == (ll & 7)
+        home_hi = dot_nt(dot_nt(mine, whi).astype(BF16), spread_a)
+        home_lo = dot_nt(dot_nt(mine, wlo).astype(BF16), spread_a)
+        mix_a[0] = jnp.where(keep, home_hi, 0.0).astype(BF16)
+        mix_a[1] = jnp.where(keep, home_lo, 0.0).astype(BF16)
+        rr = iota((64, 128), 0)
+        ll = iota((64, 128), 1)
+        gather[...] = onehot(
+            ((rr >> 5) == ((ll >> 4) & 1))
+            & (((rr >> 3) & 3) == ((ll & 15) >> 2))
+            & ((rr & 7) == (ll & 3))
+        )
+
+    down_a(0)
     b_other()
-    down_a(0)
     down_a(1)
+    chip_sum(0)
     b_mine()
-    chip_sum(0)
     down_a(2)
     chip_sum(1)
+    down_a(3)
     b_home()
-    down_a(3)
     chip_sum(2)
     chip_sum(3)
     ret_relay(0)
     ret_relay(1)
     ret_relay(2)
     ret_relay(3)
+    home_tables()
     ret_sum(0)
     ret_sum(1)
     a_home(0)
     ret_sum(2)
-
-    rr = iota((128, 256), 0)
-    ll = iota((128, 256), 1)
-    wide_hi = dot_nt(dot_nt(wide, whi).astype(BF16), spread_b)
-    wide_lo = dot_nt(dot_nt(wide, wlo).astype(BF16), spread_b)
+    a_home(1)
 
     whole(bback, 15, rbs, rbr).wait_recv()
     partial = jnp.zeros((128, 256), F32)
     for q in range(4):
-        keep = ((rr >> 4) == ((ll & 15) >> 1)) & (((rr & 15) >> 2) == q)
         piece = bback[:, :, q * 256 : q * 256 + 256].reshape(256, 256)
-        partial = partial + dot(jnp.where(keep, wide_hi, 0.0).astype(BF16), piece)
-        partial = partial + dot(jnp.where(keep, wide_lo, 0.0).astype(BF16), piece)
+        partial = partial + dot(mix_b[2 * q], piece) + dot(mix_b[2 * q + 1], piece)
     fsend[...] = partial.astype(BF16).reshape(8, 16, 256)
     frecv[tp] = fsend[tp]
 
@@ -671,40 +723,32 @@
 
     lax.fori_loop(1, 8, send_b4, 0)
     ret_sum(3)
-    a_home(1)
+    a_home(2)
+    drain()
+
+    def finish_a(h):
+        first, chunks = OUT_PARTS[h]
+        width = chunks * CHUNK // 8
+        whole(abacks[h], 15, ras.at[h], rar.at[h]).wait_recv()
+        back = abacks[h][...].reshape(256, width)
+        home_a = dot(mix_a[0], back) + dot(mix_a[1], back)
+        for p in range(8):
+            start = first * CHUNK + p * width
+            cols = slice(start, start + width)
+            out[:, cols] = (stream[0:4, cols] + home_a[p * 8 : p * 8 + 4, :]).astype(BF16)
+
+    finish_a(0)
+    finish_a(1)
     whole(frecv, 7, rfis, rfir).wait_recv()
-    rr = iota((64, 128), 0)
-    ll = iota((64, 128), 1)
-    gather = onehot(
-        ((rr >> 5) == ((ll >> 4) & 1))
-        & (((rr >> 3) & 3) == ((ll & 15) >> 2))
-        & ((rr & 7) == (ll & 3))
-    )
-    home_b = dot(gather, frecv[...].reshape(128, 256))
+    home_b = dot(gather[...], frecv[...].reshape(128, 256))
     for piece in range(8):
         start = A_COLS + piece * 256
         out[:, start : start + 256] = (
             stream[0:4, start : start + 256] + home_b[piece * 8 : piece * 8 + 4, :]
         ).astype(BF16)
-
-    rr = iota((64, 256), 0)
-    ll = iota((64, 256), 1)
-    keep = (rr >> 3) == (ll & 7)
-    home_hi = dot_nt(dot_nt(mine, whi).astype(BF16), spread_a)
-    home_lo = dot_nt(dot_nt(mine, wlo).astype(BF16), spread_a)
-    home_hi = jnp.where(keep, home_hi, 0.0).astype(BF16)
-    home_lo = jnp.where(keep, home_lo, 0.0).astype(BF16)
-
-    drain()
-    for h in range(2):
-        whole(aback.at[h], 15, ras.at[h], rar.at[h]).wait_recv()
-        back = aback[h].reshape(256, 256)
-        home_a = dot(home_hi, back) + dot(home_lo, back)
-        for p in range(8):
-            cols = slice(h * 2048 + p * 256, h * 2048 + p * 256 + 256)
-            out[:, cols] = (stream[0:4, cols] + home_a[p * 8 : p * 8 + 4, :]).astype(BF16)
-    for h in range(2):
-        whole(aback.at[h], 15, ras.at[h], rar.at[h]).wait_send()
+    finish_a(2)
+    for h, aback in enumerate(abacks):
+        whole(aback, 15, ras.at[h], rar.at[h]).wait_send()
 
 
 def layer(
@@ -768,9 +812,9 @@
         pltpu.VMEM((n, 4, 32, CHUNK), BF16),
         pltpu.VMEM((2, n, 16, CHUNK), BF16),
         pltpu.VMEM((2, n, 32, CHUNK), BF16),
-        pltpu.VMEM((2, 256, 256), BF16),
-        pltpu.VMEM((2, 16, 16, 256), BF16),
-        pltpu.VMEM((2, 16, 16, 256), BF16),
+        *[pltpu.VMEM((256, c * CHUNK // 8), BF16) for _, c in OUT_PARTS],
+        *[pltpu.VMEM((16, 16, c * CHUNK // 8), BF16) for _, c in OUT_PARTS],
+        *[pltpu.VMEM((16, 16, c * CHUNK // 8), BF16) for _, c in OUT_PARTS],
         pltpu.VMEM((256, CHUNK), BF16),
         pltpu.VMEM((256, CHUNK), F32),
         pltpu.VMEM((256, CHUNK), BF16),
@@ -778,6 +822,9 @@
         pltpu.VMEM((16, 16, CHUNK), BF16),
         pltpu.VMEM((8, 16, 256), BF16),
         pltpu.VMEM((8, 16, 256), BF16),
+        pltpu.VMEM((2, 64, 256), BF16),
+        pltpu.VMEM((8, 128, 256), BF16),
+        pltpu.VMEM((64, 128), BF16),
         dma((13,)),
         dma((2,)),
         dma((2,)),
@@ -788,19 +835,19 @@
         dma((3,)),
         dma((3,)),
         dma,
-        dma((2, n)),
-        dma,
-        dma((2, n)),
+        dma((2, IN_CHUNKS)),
+        dma,
+        dma((2, IN_CHUNKS)),
+        dma,
+        dma((IN_CHUNKS,)),
         dma,
         dma((n,)),
         dma,
         dma((n,)),
         dma,
-        dma((2, n)),
-        dma,
-        dma((2, n)),
-        dma((2,)),
-        dma((2,)),
+        dma((n,)),
+        dma((3,)),
+        dma((3,)),
         dma,
         dma,
         dma,

time: 52.2 us -> 51 us (0.977)
  Pallas kernels: 50.6 us -> 49.4 us
    pallas_call x1, Pallas kernels: 50.6 us -> 49.4 us  [layer(): pl.pallas_call(kernel, out_shape=jax.ShapeDtypeStruct((ROWS, D), BF16), i...]
where the time goes in v5:
time: 51 us; the launch traced here: 50.9 us
  Pallas kernels  49.4 us (97%)
  local copies, waits for them, and re-layouts  1.44 us (3%)
    pallas_call x1, Pallas kernels, layer(): pl.pallas_call(kernel, out_shape=jax.ShapeDtypeStruct((ROWS, D), BF16), i...  49.4 us
    unnamed x1, local copies, waits for them, and re-layouts  1.44 us

profile of v5, /device:TPU:0, one launch (start us, length us, event | category | flops | bytes accessed | tf_op | source)
XLA Modules:
  0.0 50.9 jit_solution(13598412846578823790)
XLA Ops:
  0.0 49.4 %shard_map.127 = bf16[4,6144]{1,0:T(4,128)(2,1)} custom-call(s32[4]{0:T(128)} %clen_hbm.1, bf16[4,6144]{1,0:T(4,128)(2,1)} %resid_hbm.1, bf16[4,6144]{1,0:T(4,128)(2,1)} %query_hbm.1, bf16[4,1024]{1,0:T(4,128)(2,1)} %new_key_hbm.1, bf16[4,1024]{1,0:T(4,128)(2,1)} %new_value_hbm.1, f32[1,6144]{1,0:T(1,128)} %bitcast.3, s32[4,32]{1,0:T(4,128)} %bitcast.4, ...), custom_call_target="tpu_custom_call" | custom-call | flops 6341787648 | bytes 28311552 | tf_op jit(solution)/shard_map/pallas_call | solution.py:858
  49.4 1.4 %copy.15 = bf16[4,6144]{1,0:T(4,128)(2,1)} copy(bf16[4,6144]{1,0:T(4,128)(2,1)} %shard_map.127) | data formatting | bytes 98304

commit v6 on v5

--- a/solution.py
+++ b/solution.py
@@ -285,13 +285,9 @@
     rr = iota((256, 32), 0)
     ll = iota((256, 32), 1)
     spread_a = onehot((rr >> 3) == ll)
-    spread_b = onehot(ll == ((rr >> 4) * 2 + (rr & 1)))
     rr = iota((64, 32), 0)
     ll = iota((64, 32), 1)
     mine = onehot((ll == tp * 4 + (rr & 7)) & ((rr & 7) < 4))
-    rr = iota((128, 32), 0)
-    ll = iota((128, 32), 1)
-    wide = onehot(ll == ((rr >> 4) * 4 + (rr & 3)))
     pack_a = dot_nt(spread_a, dot_nt(mine, sel).astype(BF16))
     rr = iota((256, 64), 0)
     ll = iota((256, 64), 1)
@@ -299,10 +295,6 @@
     rr = iota((16, 32), 0)
     ll = iota((16, 32), 1)
     pack_b1 = onehot(ll == (rr >> 2) * 8 + (rr & 3))
-    pack_b = dot_nt(spread_b, dot_nt(wide, sel).astype(BF16))
-    rr = iota((256, 128), 0)
-    ll = iota((256, 128), 1)
-    pack_b = jnp.where(((rr & 15) >> 1) == (ll >> 4), pack_b, 0.0)
 
     block = GROUP * ROWS
     row_of = iota((block, 128), 0) & 3
@@ -387,6 +379,16 @@
             peer, device = plane(dy * 4 + dz)
             remote(apack.at[peer], arecv.at[me], a1s.at[h], a1r.at[h], device).start()
 
+    rr = iota((256, 32), 0)
+    ll = iota((256, 32), 1)
+    spread_b = onehot(ll == ((rr >> 4) * 2 + (rr & 1)))
+    rr = iota((128, 32), 0)
+    ll = iota((128, 32), 1)
+    wide = onehot(ll == ((rr >> 4) * 4 + (rr & 3)))
+    pack_b = dot_nt(spread_b, dot_nt(wide, sel).astype(BF16))
+    rr = iota((256, 128), 0)
+    ll = iota((256, 128), 1)
+    pack_b = jnp.where(((rr & 15) >> 1) == (ll >> 4), pack_b, 0.0)
     rr = iota((256, 256), 0)
     ll = iota((256, 256), 1)
     unpack_a = onehot(ll == (rr & 31) * 8 + (rr >> 5))

time: 51 us -> 51 us (level)
  no operation moved by 1% of the time
where the time goes in v6:
time: 51 us; the launch traced here: 50.9 us
  Pallas kernels  49.4 us (97%)
  local copies, waits for them, and re-layouts  1.44 us (3%)
    pallas_call x1, Pallas kernels, layer(): pl.pallas_call(kernel, out_shape=jax.ShapeDtypeStruct((ROWS, D), BF16), i...  49.4 us
    unnamed x1, local copies, waits for them, and re-layouts  1.44 us

profile of v6, /device:TPU:0, one launch (start us, length us, event | category | flops | bytes accessed | tf_op | source)
XLA Modules:
  0.0 50.9 jit_solution(10752986407761699800)
XLA Ops:
  0.0 49.4 %shard_map.127 = bf16[4,6144]{1,0:T(4,128)(2,1)} custom-call(s32[4]{0:T(128)} %clen_hbm.1, bf16[4,6144]{1,0:T(4,128)(2,1)} %resid_hbm.1, bf16[4,6144]{1,0:T(4,128)(2,1)} %query_hbm.1, bf16[4,1024]{1,0:T(4,128)(2,1)} %new_key_hbm.1, bf16[4,1024]{1,0:T(4,128)(2,1)} %new_value_hbm.1, f32[1,6144]{1,0:T(1,128)} %bitcast.3, s32[4,32]{1,0:T(4,128)} %bitcast.4, ...), custom_call_target="tpu_custom_call" | custom-call | flops 6341787648 | bytes 28311552 | tf_op jit(solution)/shard_map/pallas_call | solution.py:860
  49.4 1.4 %copy.15 = bf16[4,6144]{1,0:T(4,128)(2,1)} copy(bf16[4,6144]{1,0:T(4,128)(2,1)} %shard_map.127) | data formatting | bytes 98304

commit v7 on v6

--- a/solution.py
+++ b/solution.py
@@ -265,22 +265,15 @@
         copy.wait()
     lane32 = iota((32, 32), 1)
     row32 = iota((32, 32), 0)
-    fixed = gates[...].astype(F32)
-    weights = fixed / jnp.sum(fixed, axis=0, keepdims=True)
     chosen = jnp.zeros((32, 32), F32)
-    weighted = jnp.zeros((32, 32), F32)
     route = routes[...]
     for k in range(4):
         same = route[k : k + 1, :] == (row32 >> 1)
         chosen = chosen + jnp.where(same, 1.0, 0.0)
-        weighted = weighted + jnp.where(same, weights[k : k + 1, :], 0.0)
     earlier = onehot(((row32 >> 2) == (lane32 >> 2)) & (row32 < lane32))
     before = dot(chosen.astype(BF16), earlier)
     picked = (chosen > 0.5) & (jnp.abs(before - (row32 & 1).astype(F32)) < 0.5)
     sel = onehot(picked)
-    wsel = jnp.where(picked, weighted, 0.0)
-    whi = wsel.astype(BF16)
-    wlo = (wsel - whi.astype(F32)).astype(BF16)
 
     rr = iota((256, 32), 0)
     ll = iota((256, 32), 1)
@@ -665,6 +658,15 @@
             remote(asend.at[peer], aback.at[me], ras.at[h], rar.at[h], device).start()
 
     def home_tables():
+        fixed = gates[...].astype(F32)
+        weights = fixed / jnp.sum(fixed, axis=0, keepdims=True)
+        weighted = jnp.zeros((32, 32), F32)
+        for k in range(4):
+            same = routes[k : k + 1, :] == (row32 >> 1)
+            weighted = weighted + jnp.where(same, weights[k : k + 1, :], 0.0)
+        wsel = weighted * sel.astype(F32)
+        whi = wsel.astype(BF16)
+        wlo = (wsel - whi.astype(F32)).astype(BF16)
         rr = iota((128, 256), 0)
         ll = iota((128, 256), 1)
         wide_hi = dot_nt(dot_nt(wide, whi).astype(BF16), spread_b)

time: 51 us -> 51 us (level)
  no operation moved by 1% of the time
where the time goes in v7:
time: 51 us; the launch traced here: 50.9 us
  Pallas kernels  49.4 us (97%)
  local copies, waits for them, and re-layouts  1.44 us (3%)
    pallas_call x1, Pallas kernels, layer(): pl.pallas_call(kernel, out_shape=jax.ShapeDtypeStruct((ROWS, D), BF16), i...  49.4 us
    unnamed x1, local copies, waits for them, and re-layouts  1.44 us

profile of v7, /device:TPU:0, one launch (start us, length us, event | category | flops | bytes accessed | tf_op | source)
XLA Modules:
  0.0 50.9 jit_solution(12613196211856601792)
XLA Ops:
  0.0 49.4 %shard_map.127 = bf16[4,6144]{1,0:T(4,128)(2,1)} custom-call(s32[4]{0:T(128)} %clen_hbm.1, bf16[4,6144]{1,0:T(4,128)(2,1)} %resid_hbm.1, bf16[4,6144]{1,0:T(4,128)(2,1)} %query_hbm.1, bf16[4,1024]{1,0:T(4,128)(2,1)} %new_key_hbm.1, bf16[4,1024]{1,0:T(4,128)(2,1)} %new_value_hbm.1, f32[1,6144]{1,0:T(1,128)} %bitcast.3, s32[4,32]{1,0:T(4,128)} %bitcast.4, ...), custom_call_target="tpu_custom_call" | custom-call | flops 6341787648 | bytes 28311552 | tf_op jit(solution)/shard_map/pallas_call | solution.py:862
  49.4 1.4 %copy.15 = bf16[4,6144]{1,0:T(4,128)(2,1)} copy(bf16[4,6144]{1,0:T(4,128)(2,1)} %shard_map.127) | data formatting | bytes 98304
